TPU v7x, 512 devices: a whole 4x4x16 slice. The times are simulated.
512 devices in a mesh: nodes: 8 (over z_lo, core), space: 64 (over x, z_hi, y).
Axes of the slice: x: 4, y: 4, z: 16 (z_hi: 4, z_lo: 4; z = z_hi * 4 + z_lo), core: 2. Of those that a mesh axis runs over, the one named last changes fastest.
Arguments:
- displacement: float32 [32, 3, 256, 64, 256], P('nodes', None, 'space'), may hold values from -4 to 4
- slot_node: int32 [32], P('nodes'), may hold values from 0 to 31, each once
- node_weight: float32 [25], replicated, may hold values from -0.05 to 0.12
- node_stiffness: float32 [25], replicated, may hold values from 0.5 to 2
- design: float32 [256, 64, 256], P('space', 'nodes'), may hold values from 0.05 to 0.95
Outputs:
- gradient: float32 [256, 64, 256], P('space', 'nodes')
Inputs may be any that keep to these rules, and one draw needn't show every extreme that they name: `slot_node`: every node 0 to 24 is held by exactly one slot; values of 25 or more mark empty slots.
All inputs are finite; a program needn't handle non-finite values.
Results may differ from a plain program's by a relative error of at most 0.0001.
Values sent between devices are 32-bit elements; how exact they have to be, the bound alone decides.
A program may use at most 128 MiB of HBM per device.

v0:
```python
import math

import jax
import jax.numpy as jnp
import numpy as np
from jax import lax
from jax.sharding import PartitionSpec as P

POISSON = 0.3
E_FLOOR = 0.001
BETA = 8.0
ETA = 0.5


def extended(cells, sides, width):
    for axis, dim in sides:
        count = lax.axis_size(axis)
        ends = count - 1
        head = lax.slice_in_dim(cells, 0, width, axis=dim)
        tail = lax.slice_in_dim(cells, cells.shape[dim] - width, cells.shape[dim], axis=dim)
        cells = jnp.concatenate(
            [
                lax.ppermute(tail, axis, [(i, (i + 1) % count) for i in range(ends)]),
                cells,
                lax.ppermute(head, axis, [((i + 1) % count, i) for i in range(ends)]),
            ],
            axis=dim,
        )
    return cells


def passed_along(value, axis, steps):
    count = lax.axis_size(axis)
    leading, last = (max(0, -steps), min(count, count - steps))
    return lax.ppermute(value, axis, [(source, source + steps) for source in range(leading, last)])


def element_matrix():
    lam = POISSON / ((1.0 + POISSON) * (1.0 - 2.0 * POISSON))
    shear = 1.0 / (2.0 * (1.0 + POISSON))
    elastic = np.zeros((6, 6))
    elastic[:3, :3] = lam
    elastic[:3, :3] += 2.0 * shear * np.eye(3)
    elastic[3:, 3:] = shear * np.eye(3)
    point = 1.0 / math.sqrt(3.0)
    stiff = np.zeros((24, 24))
    for gz in (-point, point):
        for gy in (-point, point):
            for gx in (-point, point):
                strain = np.zeros((6, 24))
                for corner in range(8):
                    sx = 2 * (corner % 2) - 1
                    sy = 2 * (corner // 2 % 2) - 1
                    sz = 2 * (corner // 4) - 1
                    fx = (1 + sx * gx) / 2
                    fy = (1 + sy * gy) / 2
                    fz = (1 + sz * gz) / 2
                    dnx = sx * fy * fz
                    dny = sy * fx * fz
                    dnz = sz * fx * fy
                    col = 3 * corner
                    strain[0, col] = dnx
                    strain[1, col + 1] = dny
                    strain[2, col + 2] = dnz
                    strain[3, col + 1] = dnz
                    strain[3, col + 2] = dny
                    strain[4, col] = dnz
                    strain[4, col + 2] = dnx
                    strain[5, col] = dny
                    strain[5, col + 1] = dnx
                stiff += strain.T @ elastic @ strain / 8.0
    return np.asarray(stiff, np.float32)


def filter_offsets():
    found = []
    for dz in range(-2, 3):
        for dy in range(-2, 3):
            for dx in range(-2, 3):
                dist = math.sqrt(dz * dz + dy * dy + dx * dx)
                if dist < 2.5:
                    found.append((dz, dy, dx, 2.5 - dist))
    return found


def smooth(padded, planes, rows, cols):
    total = jnp.zeros((planes, rows, cols), jnp.float32)
    for dz, dy, dx, weight in filter_offsets():
        total = (
            total
            + weight
            * padded[2 + dz : 2 + dz + planes, 2 + dy : 2 + dy + rows, 2 + dx : 2 + dx + cols]
        )
    return total


def project(filtered):
    base = math.tanh(BETA * ETA)
    scale = base + math.tanh(BETA * (1.0 - ETA))
    level = jnp.tanh(BETA * (filtered - ETA))
    return ((base + level) / scale, BETA * (1.0 - level * level) / scale)


def coverage(first_plane, first_row, planes, rows, cols, all_planes, all_rows):
    zpos = first_plane - 2 + jnp.arange(planes + 4, dtype=jnp.int32)
    ypos = first_row - 2 + jnp.arange(rows + 4, dtype=jnp.int32)
    zin = ((zpos >= 0) & (zpos < all_planes)).astype(jnp.float32)
    yin = ((ypos >= 0) & (ypos < all_rows)).astype(jnp.float32)
    xin = jnp.pad(jnp.ones((cols,), jnp.float32), 2)
    inside = zin[:, None, None] * yin[None, :, None] * xin[None, None, :]
    return smooth(inside, planes, rows, cols)


def element_energy(field, stiffness):
    planes = field.shape[1] - 1
    rows = field.shape[2] - 1
    cols = field.shape[3] - 1
    pieces = []
    for corner in range(8):
        a = corner % 2
        b = corner // 2 % 2
        c = corner // 4
        pieces.append(field[:, c : c + planes, b : b + rows, a : a + cols])
    vector = jnp.stack(pieces).reshape(24, planes * rows * cols)
    image = jnp.dot(
        stiffness, vector, precision=lax.Precision.HIGHEST, preferred_element_type=jnp.float32
    )
    return jnp.sum(vector * image, axis=0).reshape(planes, rows, cols)


def per_device(displacement, slot_node, node_weight, node_stiffness, design):
    stiffness = jnp.asarray(element_matrix())
    slots = displacement.shape[0]
    planes, tile_rows, cols = design.shape
    rows = displacement.shape[3]
    groups = lax.axis_size("nodes")
    group = lax.axis_index("nodes")
    slab = lax.axis_index("space")
    all_planes = planes * lax.axis_size("space")
    all_rows = tile_rows * groups
    first_plane = slab * planes
    first_row = group * tile_rows
    rim = extended(design, (("nodes", 1), ("space", 0)), 2)
    tile_cover = coverage(first_plane, first_row, planes, tile_rows, cols, all_planes, all_rows)
    filtered = smooth(jnp.pad(rim, ((0, 0), (0, 0), (2, 2))), planes, tile_rows, cols) / tile_cover
    projected, slope = project(filtered)
    ratio_tile = slope / tile_cover
    projected_slab, ratio_slab = (
        lax.all_gather(projected, "nodes", axis=1, tiled=True),
        lax.all_gather(ratio_tile, "nodes", axis=1, tiled=True),
    )
    upper = passed_along(displacement[:, :, :1], "space", -1)
    field_all = jnp.concatenate([displacement, upper], axis=2)
    field_all = jnp.pad(field_all, ((0, 0), (0, 0), (0, 0), (0, 1), (0, 1)))
    picks = (
        slot_node[:, None] == jnp.arange(node_weight.shape[0], dtype=jnp.int32)[None, :]
    ).astype(jnp.float32)
    coef = jnp.sum(picks * (node_weight * node_stiffness)[None, :], axis=1)

    def add_slot(slot, total):
        field = lax.dynamic_index_in_dim(field_all, slot, 0, keepdims=False)
        return total + coef[slot] * element_energy(field, stiffness)

    total = lax.fori_loop(0, slots, add_slot, jnp.zeros((planes, rows, cols), jnp.float32))
    sens_slab = -3.0 * (1.0 - E_FLOOR) * (projected_slab * projected_slab) * total
    sens_tile = lax.psum_scatter(sens_slab, "nodes", scatter_dimension=1, tiled=True)
    scaled = sens_tile * ratio_tile
    rim_sens = extended(scaled, (("nodes", 1), ("space", 0)), 2)
    gradient = smooth(jnp.pad(rim_sens, ((0, 0), (0, 0), (2, 2))), planes, tile_rows, cols)
    return gradient


def solution(mesh):
    return jax.shard_map(
        per_device,
        mesh=mesh,
        in_specs=(
            P("nodes", None, "space", None, None),
            P("nodes"),
            P(),
            P(),
            P("space", "nodes", None),
        ),
        out_specs=P("space", "nodes", None),
        check_vma=False,
    )
```

profile of v0, /device:TPU:7, one launch (start us, length us, event | category | flops | bytes accessed | tf_op | source)
XLA Modules:
  0.0 307.9 jit_solution(3531750600159734128)
XLA Ops:
  6.5 1.2 slice.1065
  7.8 15.2 %collective-permute-start.4 = (f32[4,3,1,64,256]{4,3,2,1,0:T(8,128)S(1)}, f32[4,3,1,64,256]{4,3,2,1,0:T(8,128)S(1)}, u32[]{:S(2)}, u32[]{:S(2)}) collective-permute-start(f32[4,3,1,64,256]{4,3,2,1,0:T(8,128)S(1)} %slice.1065), channel_id=1, source_target_pairs={{1,0},{2,1},{3,2},{4,3},{5,4},{6,5},{7,6},{8,7},{9,8},{10,9},{11,1... | collective-permute-start | bytes 2359304 | tf_op jit(solution)/shard_map/ppermute | solution.py:35
  23.8 2.9 collective-permute-start.1
  26.6 2.7 collective-permute-start
  31.9 59.9 %collective-permute-done.1 = f32[4,2,256]{2,1,0:T(2,128)S(1)} collective-permute-done((f32[4,2,256]{2,1,0:T(2,128)S(1)}, f32[4,2,256]{2,1,0:T(2,128)S(1)}, u32[]{:S(2)}, u32[]{:S(2)}) %collective-permute-start.1) | collective-permute-done | bytes 8224 | tf_op jit(solution)/shard_map/ppermute | solution.py:25
  92.6 1.9 collective-permute-start.3
  94.5 3.4 %collective-permute-start.2 = (f32[2,12,256]{2,1,0:T(8,128)S(1)}, f32[2,12,256]{2,1,0:T(8,128)S(1)}, u32[]{:S(2)}, u32[]{:S(2)}) collective-permute-start(f32[2,12,256]{2,1,0:T(8,128)S(1)} %get-tuple-element.143), channel_id=1, source_target_pairs={{0,1},{1,2},{2,3},{3,4},{4,5},{5,6},{6,7},{7,8},{8,9},{9,10},{10,1... | collective-permute-start | bytes 73736 | tf_op jit(solution)/shard_map/ppermute | solution.py:23
  97.9 8.2 %collective-permute-done.2 = f32[2,12,256]{2,1,0:T(8,128)S(1)} collective-permute-done((f32[2,12,256]{2,1,0:T(8,128)S(1)}, f32[2,12,256]{2,1,0:T(8,128)S(1)}, u32[]{:S(2)}, u32[]{:S(2)}) %collective-permute-start.2) | collective-permute-done | bytes 24608 | tf_op jit(solution)/shard_map/ppermute | solution.py:23
  107.8 2.0 add_multiply_fusion
  109.8 13.0 %all_gather.3 = f32[4,64,256]{2,1,0:T(8,128)S(1)} all-gather(f32[4,8,256]{2,1,0:T(8,128)S(1)} %get-tuple-element.138), channel_id=1, replica_groups=mesh['nodes'=8,'space'=64] {'nodes'}, dimensions={1}, use_global_device_ids=true | all-gather | bytes 294912 | tf_op jit(solution)/shard_map/all_gather | solution.py:149
  122.9 3.0 select_maximum_fusion
  125.9 113.7 %while.15 = (s32[]{:T(128)}, f32[4,64,256]{2,1,0:T(8,128)S(1)}, f32[4]{0:T(128)S(1)}, f32[4,3,5,65,257]{4,3,2,1,0:T(8,128)}, s32[]{:T(128)}, /*index=5*/f32[24,24]{1,0:T(8,128)S(1)}, s32[]{:T(128)}) while((s32[]{:T(128)}, f32[4,64,256]{2,1,0:T(8,128)S(1)}, f32[4]{0:T(128)S(1)}, f32[4,3,5,65,257]{4,3,2,1,0:T(8,128)}, ...), condition=%wide.region_3.4_spmd.clone.clone, body=%wide.region_1.3_spmd.sunk.clone.clone.sunk | while | flops 456261632 | bytes 35561448 | solution.py:164
  125.9 1.5 dynamic-slice_bitcast_fusion.2
  134.9 1.2 fusion.291
  136.0 6.9 %reshape.69 = f32[24,65536]{1,0:T(8,128)} reshape(f32[8,3,4,64,256]{4,3,2,1,0:T(8,128)} %fusion.291) | data formatting | bytes 12582912 | tf_op jit(solution)/shard_map/while/body/eval_jaxpr/reshape | solution.py:124
  142.9 9.9 %fusion.292 = f32[65536]{0:T(1024)S(1)} fusion(f32[24,65536]{1,0:T(8,128)} %reshape.69, f32[24,24]{1,0:T(8,128)S(1)} %get-tuple-element.197), kind=kOutput, calls=%fused_computation.1.clone.1 | convolution fusion | flops 456065024 | bytes 6555904 | tf_op jit(solution)/shard_map/while/body/eval_jaxpr/dot_general | solution.py:125
  154.3 1.5 dynamic-slice_bitcast_fusion.2
  163.3 1.2 fusion.291
  164.5 6.9 %reshape.69 = f32[24,65536]{1,0:T(8,128)} reshape(f32[8,3,4,64,256]{4,3,2,1,0:T(8,128)} %fusion.291) | data formatting | bytes 12582912 | tf_op jit(solution)/shard_map/while/body/eval_jaxpr/reshape | solution.py:124
  171.4 9.9 %fusion.292 = f32[65536]{0:T(1024)S(1)} fusion(f32[24,65536]{1,0:T(8,128)} %reshape.69, f32[24,24]{1,0:T(8,128)S(1)} %get-tuple-element.197), kind=kOutput, calls=%fused_computation.1.clone.1 | convolution fusion | flops 456065024 | bytes 6555904 | tf_op jit(solution)/shard_map/while/body/eval_jaxpr/dot_general | solution.py:125
  182.7 1.5 dynamic-slice_bitcast_fusion.2
  192.9 6.9 %reshape.69 = f32[24,65536]{1,0:T(8,128)} reshape(f32[8,3,4,64,256]{4,3,2,1,0:T(8,128)} %fusion.291) | data formatting | bytes 12582912 | tf_op jit(solution)/shard_map/while/body/eval_jaxpr/reshape | solution.py:124
  199.8 9.9 %fusion.292 = f32[65536]{0:T(1024)S(1)} fusion(f32[24,65536]{1,0:T(8,128)} %reshape.69, f32[24,24]{1,0:T(8,128)S(1)} %get-tuple-element.197), kind=kOutput, calls=%fused_computation.1.clone.1 | convolution fusion | flops 456065024 | bytes 6555904 | tf_op jit(solution)/shard_map/while/body/eval_jaxpr/dot_general | solution.py:125
  211.2 1.5 dynamic-slice_bitcast_fusion.2
  221.4 6.9 %reshape.69 = f32[24,65536]{1,0:T(8,128)} reshape(f32[8,3,4,64,256]{4,3,2,1,0:T(8,128)} %fusion.291) | data formatting | bytes 12582912 | tf_op jit(solution)/shard_map/while/body/eval_jaxpr/reshape | solution.py:124
  228.2 9.9 %fusion.292 = f32[65536]{0:T(1024)S(1)} fusion(f32[24,65536]{1,0:T(8,128)} %reshape.69, f32[24,24]{1,0:T(8,128)S(1)} %get-tuple-element.197), kind=kOutput, calls=%fused_computation.1.clone.1 | convolution fusion | flops 456065024 | bytes 6555904 | tf_op jit(solution)/shard_map/while/body/eval_jaxpr/dot_general | solution.py:125
  240.4 30.0 %reduce-scatter.2.cloned.1.call-done = f32[4,8,256]{2,1,0:T(8,128)} async-done(((f32[4,64,256]{2,1,0:T(8,128)}), f32[4,8,256]{2,1,0:T(8,128)}) %reduce-scatter.2.cloned.1.call-update) | async-done | bytes 32784 | tf_op jit(solution)/shard_map/reduce_scatter | solution.py:166
  271.2 6.0 %collective-permute-start.6 = (f32[4,2,256]{2,1,0:T(2,128)S(1)}, f32[4,2,256]{2,1,0:T(2,128)S(1)}, u32[]{:S(2)}, u32[]{:S(2)}) collective-permute-start(f32[4,2,256]{2,1,0:T(2,128)S(1)} %get-tuple-element.150), channel_id=1, source_target_pairs={{64,0},{128,64},{192,128},{256,192},{320,256},{384,320},{448,384},... | collective-permute-start | bytes 24584 | tf_op jit(solution)/shard_map/ppermute | solution.py:25
  277.2 1.9 collective-permute-start.5
  280.3 7.9 %collective-permute-start.8 = (f32[2,12,256]{2,1,0:T(8,128)S(1)}, f32[2,12,256]{2,1,0:T(8,128)S(1)}, u32[]{:S(2)}, u32[]{:S(2)}) collective-permute-start(f32[2,12,256]{2,1,0:T(8,128)S(1)} %get-tuple-element.142), channel_id=1, source_target_pairs={{1,0},{2,1},{3,2},{4,3},{5,4},{6,5},{7,6},{8,7},{9,8},{10,9},{11,1... | collective-permute-start | bytes 73736 | tf_op jit(solution)/shard_map/ppermute | solution.py:25
  288.2 1.9 collective-permute-start.7
  290.1 9.6 %collective-permute-done.7 = f32[2,12,256]{2,1,0:T(8,128)S(1)} collective-permute-done((f32[2,12,256]{2,1,0:T(8,128)S(1)}, f32[2,12,256]{2,1,0:T(8,128)S(1)}, u32[]{:S(2)}, u32[]{:S(2)}) %collective-permute-start.7) | collective-permute-done | bytes 24608 | tf_op jit(solution)/shard_map/ppermute | solution.py:23
  (82 shorter events, 47.6 us)
Async XLA Ops:
  6.5 263.9 %reduce-scatter.2.cloned.1.call-start = ((), (), s32[]{:S(2)}) async-start(), calls=%async_computation.1 | async-start | bytes 294912 | tf_op jit(solution)/shard_map/reduce_scatter | solution.py:166
  7.8 115.1 %collective-permute-start.4 = (f32[4,3,1,64,256]{4,3,2,1,0:T(8,128)S(1)}, f32[4,3,1,64,256]{4,3,2,1,0:T(8,128)S(1)}, u32[]{:S(2)}, u32[]{:S(2)}) collective-permute-start(f32[4,3,1,64,256]{4,3,2,1,0:T(8,128)S(1)} %slice.1065), channel_id=1, source_target_pairs={{1,0},{2,1},{3,2},{4,3},{5,4},{6,5},{7,6},{8,7},{9,8},{10,9},{11,1... | collective-permute-start | bytes 2359304 | tf_op jit(solution)/shard_map/ppermute | solution.py:35
  23.8 68.0 %collective-permute-start.1 = (f32[4,2,256]{2,1,0:T(2,128)S(1)}, f32[4,2,256]{2,1,0:T(2,128)S(1)}, u32[]{:S(2)}, u32[]{:S(2)}) collective-permute-start(f32[4,2,256]{2,1,0:T(2,128)S(1)} %get-tuple-element.152), channel_id=1, source_target_pairs={{64,0},{128,64},{192,128},{256,192},{320,256},{384,320},{448,384},... | collective-permute-start | bytes 24584 | tf_op jit(solution)/shard_map/ppermute | solution.py:25
  26.6 65.1 %collective-permute-start = (f32[4,2,256]{2,1,0:T(2,128)S(1)}, f32[4,2,256]{2,1,0:T(2,128)S(1)}, u32[]{:S(2)}, u32[]{:S(2)}) collective-permute-start(f32[4,2,256]{2,1,0:T(2,128)S(1)} %get-tuple-element.151), channel_id=1, source_target_pairs={{0,64},{64,128},{128,192},{192,256},{256,320},{320,384},{384,448},... | collective-permute-start | bytes 24584 | tf_op jit(solution)/shard_map/ppermute | solution.py:23
  31.9 91.0 %copy-start = (f32[4,3,4,64,256]{4,3,2,1,0:T(8,128)S(1)}, f32[4,3,4,64,256]{4,3,2,1,0:T(8,128)}, u32[]{:S(2)}) copy-start(f32[4,3,4,64,256]{4,3,2,1,0:T(8,128)} %param.8) | copy-start | bytes 9437188
  92.6 5.3 %collective-permute-start.3 = (f32[2,12,256]{2,1,0:T(8,128)S(1)}, f32[2,12,256]{2,1,0:T(8,128)S(1)}, u32[]{:S(2)}, u32[]{:S(2)}) collective-permute-start(f32[2,12,256]{2,1,0:T(8,128)S(1)} %get-tuple-element.144), channel_id=1, source_target_pairs={{1,0},{2,1},{3,2},{4,3},{5,4},{6,5},{7,6},{8,7},{9,8},{10,9},{11,1... | collective-permute-start | bytes 73736 | tf_op jit(solution)/shard_map/ppermute | solution.py:25
  94.5 11.6 %collective-permute-start.2 = (f32[2,12,256]{2,1,0:T(8,128)S(1)}, f32[2,12,256]{2,1,0:T(8,128)S(1)}, u32[]{:S(2)}, u32[]{:S(2)}) collective-permute-start(f32[2,12,256]{2,1,0:T(8,128)S(1)} %get-tuple-element.143), channel_id=1, source_target_pairs={{0,1},{1,2},{2,3},{3,4},{4,5},{5,6},{6,7},{7,8},{8,9},{9,10},{10,1... | collective-permute-start | bytes 73736 | tf_op jit(solution)/shard_map/ppermute | solution.py:23
  109.8 16.0 %copy-start.1 = (f32[24,24]{1,0:T(8,128)S(1)}, f32[24,24]{1,0:T(8,128)}, u32[]{:S(2)}) copy-start(f32[24,24]{1,0:T(8,128)} %constant.95.clone..sunk.3) | copy-start | bytes 6916
  271.2 7.9 %collective-permute-start.6 = (f32[4,2,256]{2,1,0:T(2,128)S(1)}, f32[4,2,256]{2,1,0:T(2,128)S(1)}, u32[]{:S(2)}, u32[]{:S(2)}) collective-permute-start(f32[4,2,256]{2,1,0:T(2,128)S(1)} %get-tuple-element.150), channel_id=1, source_target_pairs={{64,0},{128,64},{192,128},{256,192},{320,256},{384,320},{448,384},... | collective-permute-start | bytes 24584 | tf_op jit(solution)/shard_map/ppermute | solution.py:25
  277.2 3.1 collective-permute-start.5
  280.3 9.8 %collective-permute-start.8 = (f32[2,12,256]{2,1,0:T(8,128)S(1)}, f32[2,12,256]{2,1,0:T(8,128)S(1)}, u32[]{:S(2)}, u32[]{:S(2)}) collective-permute-start(f32[2,12,256]{2,1,0:T(8,128)S(1)} %get-tuple-element.142), channel_id=1, source_target_pairs={{1,0},{2,1},{3,2},{4,3},{5,4},{6,5},{7,6},{8,7},{9,8},{10,9},{11,1... | collective-permute-start | bytes 73736 | tf_op jit(solution)/shard_map/ppermute | solution.py:25
  288.2 11.6 %collective-permute-start.7 = (f32[2,12,256]{2,1,0:T(8,128)S(1)}, f32[2,12,256]{2,1,0:T(8,128)S(1)}, u32[]{:S(2)}, u32[]{:S(2)}) collective-permute-start(f32[2,12,256]{2,1,0:T(8,128)S(1)} %get-tuple-element.141), channel_id=1, source_target_pairs={{0,1},{1,2},{2,3},{3,4},{4,5},{5,6},{6,7},{7,8},{8,9},{9,10},{10,1... | collective-permute-start | bytes 73736 | tf_op jit(solution)/shard_map/ppermute | solution.py:23
Sparse Core Ops, SparseCore 0:
  240.5 29.8 reduce-scatter.1
where the time goes:
time: 311 us; the launch traced here: 308 us
  waiting for transfers between devices  109 us (35%)
  local copies, waits for them, and re-layouts  73.8 us (24%)
  starting transfers between devices  43.7 us (14%)
  matrix products  39.8 us (13%)
  other arithmetic  14.9 us (5%)
  between operations  13.6 us (4%)
  blocking collectives  13 us (4%)
    ppermute x4, waiting for transfers between devices, extended(): lax.ppermute(head, axis, [((i + 1) % count, i) for i in range(ends)])  59.9 us
    dot_general x4, matrix products, element_energy(): jnp.dot(stiffness, vector, precision=lax.Precision.HIGHEST, preferred_ele...  39.8 us
    reduce_scatter x1, waiting for transfers between devices, per_device(): lax.psum_scatter(sens_slab, 'nodes', scatter_dimension=1, tiled=True)  30 us
    while x28, local copies, waits for them, and re-layouts  29.7 us
    reshape x4, local copies, waits for them, and re-layouts, element_energy(): vector = jnp.stack(pieces).reshape(24, planes * rows * cols)  27.5 us
    ppermute x4, waiting for transfers between devices, extended(): lax.ppermute(tail, axis, [(i, (i + 1) % count) for i in range(ends)])  18.9 us
    ppermute x4, starting transfers between devices, extended(): lax.ppermute(head, axis, [((i + 1) % count, i) for i in range(ends)])  18.6 us
    ppermute x1, starting transfers between devices, passed_along(): lax.ppermute(value, axis, [(source, source + steps) for source in range(l...  15.2 us
  transfers between devices with their start and end apart: 10, of which 5 were waited for; matrix products, arithmetic and copies ran while one was open for 3% of the time, Pallas kernels for 0%

commit v1 on v0

v1 whole, which is shorter than its diff:
```python
import math

import jax
import jax.numpy as jnp
from jax import lax
from jax.experimental import pallas as pl
from jax.experimental.pallas import tpu as pltpu
from jax.sharding import PartitionSpec as P

POISSON = 0.3
E_FLOOR = 0.001
BETA = 8.0
ETA = 0.5
RADIUS = 2.5
MESH = pl.DeviceIdType.MESH


def weight(dz, dy, dx):
    return max(0.0, RADIUS - math.sqrt(dz * dz + dy * dy + dx * dx))


def add_up(terms):
    total = None
    for term in terms:
        total = term if total is None else total + term
    return total


def next_lane(v, last):
    return jnp.where(last, 0.0, pltpu.roll(v, v.shape[1] - 1, 1))


def plane_modes(load, next_rows, last):
    modes = []
    for comp in range(3):
        here, below = load(comp)
        up = pltpu.roll(jnp.where(next_rows, below, here), 7, 0)
        ysum, ydif = up + here, up - here
        ysum_x, ydif_x = next_lane(ysum, last), next_lane(ydif, last)
        modes.append((ysum_x + ysum, ysum_x - ysum, ydif_x + ydif, ydif_x - ydif))
    return modes


def layer_energy(low, high):
    lam = POISSON / ((1.0 + POISSON) * (1.0 - 2.0 * POISSON))
    shear = 1.0 / (2.0 * (1.0 + POISSON))
    sums = [[lo + hi for lo, hi in zip(a, b)] for a, b in zip(low, high)]
    difs = [[hi - lo for lo, hi in zip(a, b)] for a, b in zip(low, high)]
    (_, ax, ay, axy), (_, bx, by, bxy), (_, cx, cy, cxy) = sums
    (az, azx, ayz, axyz), (bz, bzx, byz, bxyz), (cz, czx, cyz, cxyz) = difs
    sq = lambda v: v * v
    div = sq(ax + by + cz)
    diag = sq(ax) + sq(by) + sq(cz)
    skew = sq(ay + bx) + sq(az + cx) + sq(bz + cy)
    even = sq(bxy + czx) + sq(axy + cyz) + sq(azx + byz)
    odd = sq(bxy - czx) + sq(axy - cyz) + sq(azx - byz)
    mixed = sq(ayz + bzx) + sq(ayz + cxy) + sq(bzx + cxy)
    high_order = sq(axyz) + sq(bxyz) + sq(cxyz)
    return (
        (lam / 16.0) * div
        + (2.0 * shear / 16.0) * diag
        + (shear / 16.0) * skew
        + ((lam + 1.5 * shear) / 48.0) * even
        + (1.5 * shear / 48.0) * odd
        + (shear / 48.0) * mixed
        + ((lam + 4.0 * shear) / 144.0) * high_order
    )


def smooth(windows, cols):
    lanes = lax.broadcasted_iota(jnp.int32, windows[0][0].shape, 1)
    total = None
    for dx in range(3):
        part = add_up(
            [weight(i, j, dx) * windows[i][j] for i in range(3) for j in range(3) if weight(i, j, dx) > 0.0]
        )
        if dx > 0:
            right = jnp.where(lanes < cols - dx, pltpu.roll(part, cols - dx, 1), 0.0)
            left = jnp.where(lanes >= dx, pltpu.roll(part, dx, 1), 0.0)
            part = left + right
        total = part if total is None else total + part
    return total


def row_sums(field, plane):
    at = lambda first: field[plane, first : first + 8, :]
    return [at(8), at(7) + at(9), at(6) + at(10)]


def z_sums(rows, plane):
    return [
        rows[plane],
        [a + b for a, b in zip(rows[plane - 1], rows[plane + 1])],
        [a + b for a, b in zip(rows[plane - 2], rows[plane + 2])],
    ]


def make_kernel(groups, slabs, slots, planes, rows, cols, tile):
    half = slots // 2
    chips = groups // 2
    below = planes + 1

    def kernel(
        disp, slot_node, node_weight, node_stiffness, design, out,
        field, low_face, high_face, sums, sibling, pair, arrived,
        des_edge, des_z, des_y, des_c, fac, fac_low,
        sen, sen_edge, sen_low, sen_high, sen_y, sen_cl, sen_ch, pad,
        load_sem, send_sem, recv_sem,
    ):
        group = lax.axis_index("nodes")
        slab = lax.axis_index("space")
        core = lax.rem(group, 2)
        chip = lax.div(group, 2)
        down = lax.rem(slab + slabs - 1, slabs)
        up = lax.rem(slab + 1, slabs)
        has_prev, has_next = group > 0, group < groups - 1
        slab_low = jnp.where(slab > 0, 1.0, 0.0).astype(jnp.float32)
        slab_high = jnp.where(slab < slabs - 1, 1.0, 0.0).astype(jnp.float32)
        mate = (group + 1 - 2 * core, slab)
        peers = [(2 * lax.rem(chip + k, chips) + core, slab) for k in range(1, chips)]

        def when(condition, action):
            if condition is None:
                action()
            else:
                pl.when(condition)(action)

        aside = group + 2 * core - 1
        partners = [(mate, None), ((group, down), None), ((group, up), None)]
        partners += [(peer, None) for peer in peers]
        partners.append(((aside, slab), (aside >= 0) & (aside < groups)))
        for cond, step in ((has_prev, -1), (has_next, 1)):
            partners += [((group + step, where), cond) for where in (down, up)]
        barrier = pltpu.get_barrier_semaphore()
        for device, cond in partners:
            when(cond, lambda: pl.semaphore_signal(barrier, inc=1, device_id=device, device_id_type=MESH))

        loads = []
        for slot in range(slots):
            load = pltpu.make_async_copy(
                disp.at[slot], field.at[slot, :, :, pl.ds(0, rows), :], load_sem.at[slot]
            )
            load.start()
            loads.append(load)
        zero_rows = jnp.zeros((8, cols), jnp.float32)
        for comp in range(3):
            for slot in range(slots):
                for plane in range(planes):
                    field[slot, comp, plane, rows : rows + 8, :] = zero_rows
            for slot in range(half):
                low_face[slot, comp, rows : rows + 8, :] = zero_rows
                high_face[slot, comp, rows : rows + 8, :] = zero_rows
        des_edge[0] = design[:, 0:2, :]
        des_edge[1] = design[:, tile - 2 : tile, :]

        pl.semaphore_wait(barrier, sum(1 if cond is None else cond.astype(jnp.int32) for _, cond in partners))

        count = [0]

        def remote(src, dst, device):
            number = count[0]
            count[0] += 1
            return pltpu.make_async_remote_copy(
                src_ref=src, dst_ref=dst, send_sem=send_sem.at[number], recv_sem=recv_sem.at[number],
                device_id=device, device_id_type=MESH,
            )

        def halo(edge, z_src, z_dst, y_dst, c_dst):
            copies = []
            for side, where in ((0, down), (1, up)):
                copies.append((remote(z_src[side], z_dst[side], (group, where)), None, None))
            for rim, (step, send_if, recv_if) in enumerate(((-1, has_prev, has_next), (1, has_next, has_prev))):
                copies.append((remote(edge.at[rim], y_dst.at[rim], (group + step, slab)), send_if, recv_if))
                for side, where in ((0, down), (1, up)):
                    part = edge.at[rim, pl.ds(*((0, edge.shape[1] - 2) if side == 0 else (edge.shape[1] - 2, 2)))]
                    copies.append((remote(part, c_dst[side].at[rim], (group + step, where)), send_if, recv_if))
            return copies

        def start_all(copies):
            for copy, send_if, _ in copies:
                when(send_if, copy.start)

        def wait_all(copies):
            for copy, send_if, recv_if in copies:
                when(recv_if, copy.wait_recv)
                when(send_if, copy.wait_send)

        design_halo = halo(
            des_edge,
            (design.at[pl.ds(0, 2)], design.at[pl.ds(planes - 2, 2)]),
            (des_z.at[1], des_z.at[0]),
            des_y,
            (des_c.at[1], des_c.at[0]),
        )
        start_all(design_halo)
        to_down, to_up = [], []
        for slot in range(half):
            to_down.append(
                remote(disp.at[slot, :, 0], high_face.at[slot, :, pl.ds(0, rows), :], (group, down))
            )
            to_down[-1].start()
            to_up.append(
                remote(
                    disp.at[half + slot, :, planes - 1], low_face.at[slot, :, pl.ds(0, rows), :], (group, up)
                )
            )
            to_up[-1].start()

        coef = []
        for slot in range(slots):
            node = slot_node[slot]
            index = jnp.clip(node, 0, node_weight.shape[0] - 1)
            value = node_weight[index] * node_stiffness[index]
            coef.append(jnp.where(node < node_weight.shape[0], value, 0.0))

        last = lax.broadcasted_iota(jnp.int32, (8, cols), 1) == cols - 1
        next_rows = lax.broadcasted_iota(jnp.int32, (8, cols), 0) == 0

        def modes_of(plane_ref, block, gain=None):
            def load(comp):
                pair_of = [
                    plane_ref[comp, pl.ds(pl.multiple_of((block + k) * 8, 8), 8), :] for k in range(2)
                ]
                return pair_of if gain is None else [v * gain for v in pair_of]

            return plane_modes(load, next_rows, last)

        for slot in range(slots):
            loads[slot].wait()

            def block_step(block, carry):
                here = modes_of(field.at[slot, :, 0], block)
                for layer in range(planes - 1):
                    above = modes_of(field.at[slot, :, layer + 1], block)
                    value = coef[slot] * layer_energy(here, above)
                    place = (lax.rem(block, 2), lax.div(block, 2), layer + 1)
                    sums[place] = value if slot == 0 else sums[place] + value
                    here = above
                return carry

            lax.fori_loop(0, rows // 8, block_step, 0)

        wait_all(design_halo)
        pad[pl.ds(2, planes), pl.ds(8, tile), :] = design[...]
        pad[pl.ds(0, 2), pl.ds(8, tile), :] = des_z[0] * slab_low
        pad[pl.ds(planes + 2, 2), pl.ds(8, tile), :] = des_z[1] * slab_high
        for rim, (first, cond) in enumerate(((16, has_next), (6, has_prev))):
            inside = lambda v: jnp.where(cond, v, 0.0)
            pad[pl.ds(2, planes), pl.ds(first, 2), :] = inside(des_y[rim])
            pad[pl.ds(0, 2), pl.ds(first, 2), :] = inside(des_c[0, rim]) * slab_low
            pad[pl.ds(planes + 2, 2), pl.ds(first, 2), :] = inside(des_c[1, rim]) * slab_high

        row_at = lax.broadcasted_iota(jnp.int32, (tile, cols), 0) + group * tile
        ones = []
        for dy in range(3):
            within = lambda y: jnp.where((y >= 0) & (y < groups * tile), 1.0, 0.0)
            ones.append(within(row_at) if dy == 0 else within(row_at - dy) + within(row_at + dy))
        base = math.tanh(BETA * ETA)
        scale = base + math.tanh(BETA * (1.0 - ETA))
        filt_rows = [row_sums(pad, p) for p in range(planes + 4)]
        for plane in range(planes):
            z = slab * planes + plane
            here = lambda d: jnp.where((z + d >= 0) & (z + d < slabs * planes), 1.0, 0.0)
            gains = [1.0, here(-1) + here(1), here(-2) + here(2)]
            cover = smooth([[v * gain for v in ones] for gain in gains], cols)
            filtered = smooth(z_sums(filt_rows, plane + 2), cols) / cover
            level = jnp.tanh(BETA * (filtered - ETA))
            projected = (base + level) / scale
            slope = BETA * (1.0 - level * level) / scale
            fac[plane] = (-3.0 * (1.0 - E_FLOOR)) * (projected * projected) * slope / cover
        factor_up = remote(fac.at[planes - 1], fac_low, (group, up))
        factor_up.start()

        for slot in range(half):
            to_up[slot].wait_recv()
            to_down[slot].wait_recv()

            def face_step(block, carry):
                place = lambda layer: (lax.rem(block, 2), lax.div(block, 2), layer)
                lower = layer_energy(
                    modes_of(low_face.at[slot], block),
                    modes_of(field.at[half + slot, :, 0], block, slab_low),
                )
                value = coef[half + slot] * lower
                sums[place(0)] = value if slot == 0 else sums[place(0)] + value
                upper = layer_energy(
                    modes_of(field.at[slot, :, planes - 1], block),
                    modes_of(high_face.at[slot], block, slab_high),
                )
                value = coef[slot] * upper
                sums[place(planes)] = value if slot == 0 else sums[place(planes)] + value
                return carry

            lax.fori_loop(0, rows // 8, face_step, 0)

        swap = remote(sums.at[1 - core], sibling, mate)
        swap.start()
        swap.wait_recv()
        for index in range(chips):
            pair[index] = sums[core, index] + sibling[index]
        spread = []
        for k in range(1, chips):
            spread.append(remote(pair.at[lax.rem(chip + k, chips)], arrived.at[k - 1], peers[k - 1]))
            spread[-1].start()
        factor_up.wait_recv()
        for copy in spread:
            copy.wait_recv()
        for plane in range(below):
            total = pair[chip, plane] + add_up([arrived[k, plane] for k in range(chips - 1)])
            sen[plane] = total * (fac_low[...] if plane == 0 else fac[plane - 1])
        sen_edge[0] = sen[:, 0:2, :]
        sen_edge[1] = sen[:, tile - 2 : tile, :]

        sens_halo = halo(
            sen_edge,
            (sen.at[pl.ds(0, 3)], sen.at[pl.ds(below - 2, 2)]),
            (sen_high, sen_low),
            sen_y,
            (sen_ch, sen_cl),
        )
        start_all(sens_halo)
        wait_all(sens_halo)

        def place_rows(first, own, lower, upper):
            span = pl.ds(first, own.shape[1])
            pad[0, span, :] = lower[0] * slab_low
            pad[1, span, :] = (lower[1] + own[0]) * slab_low
            for plane in range(planes - 1):
                pad[2 + plane, span, :] = own[1 + plane]
            pad[1 + planes, span, :] = own[planes] + upper[0]
            pad[2 + planes, span, :] = upper[1] * slab_high
            pad[3 + planes, span, :] = upper[2] * slab_high

        place_rows(8, sen[...], sen_low[...], sen_high[...])
        for rim, (first, cond) in enumerate(((16, has_next), (6, has_prev))):
            inside = lambda v: jnp.where(cond, v, 0.0)
            place_rows(first, inside(sen_y[rim]), inside(sen_cl[rim]), inside(sen_ch[rim]))
        sens_rows = [row_sums(pad, p) for p in range(planes + 4)]
        for plane in range(planes):
            out[plane] = smooth(z_sums(sens_rows, plane + 2), cols)

        swap.wait_send()
        factor_up.wait_send()
        for copy in spread + to_up + to_down:
            copy.wait_send()

    vmem = lambda *shape: pltpu.VMEM(shape, jnp.float32)
    copies = 8 + 2 * half + 1 + 1 + (chips - 1) + 8
    scratch = [
        vmem(slots, 3, planes, rows + 8, cols),
        vmem(half, 3, rows + 8, cols),
        vmem(half, 3, rows + 8, cols),
        vmem(2, chips, below, tile, cols),
        vmem(chips, below, tile, cols),
        vmem(chips, below, tile, cols),
        vmem(chips - 1, below, tile, cols),
        vmem(2, planes, 2, cols),
        vmem(2, 2, tile, cols),
        vmem(2, planes, 2, cols),
        vmem(2, 2, 2, 2, cols),
        vmem(planes, tile, cols),
        vmem(tile, cols),
        vmem(below, tile, cols),
        vmem(2, below, 2, cols),
        vmem(2, tile, cols),
        vmem(3, tile, cols),
        vmem(2, below, 2, cols),
        vmem(2, 2, 2, cols),
        vmem(2, 3, 2, cols),
        vmem(planes + 4, 24, cols),
        pltpu.SemaphoreType.DMA((slots,)),
        pltpu.SemaphoreType.DMA((copies,)),
        pltpu.SemaphoreType.DMA((copies,)),
    ]
    return kernel, scratch


def solution(mesh):
    groups, slabs = mesh.shape["nodes"], mesh.shape["space"]

    def per_device(displacement, slot_node, node_weight, node_stiffness, design):
        slots, _, planes, rows, cols = displacement.shape
        kernel, scratch = make_kernel(groups, slabs, slots, planes, rows, cols, design.shape[1])
        smem = pl.BlockSpec(memory_space=pltpu.SMEM)
        vmem = pl.BlockSpec(memory_space=pltpu.VMEM)
        return pl.pallas_call(
            kernel,
            out_shape=jax.ShapeDtypeStruct(design.shape, jnp.float32),
            in_specs=[pl.BlockSpec(memory_space=pl.ANY), smem, smem, smem, vmem],
            out_specs=vmem,
            scratch_shapes=scratch,
            compiler_params=pltpu.CompilerParams(
                collective_id=0, has_side_effects=True, vmem_limit_bytes=48 * 2**20
            ),
            cost_estimate=pl.CostEstimate(flops=40_000_000, bytes_accessed=4_000_000, transcendentals=8192),
            name="sensitivity",
        )(displacement, slot_node, node_weight, node_stiffness, design)

    return jax.shard_map(
        per_device,
        mesh=mesh,
        in_specs=(
            P("nodes", None, "space", None, None),
            P("nodes"),
            P(),
            P(),
            P("space", "nodes", None),
        ),
        out_specs=P("space", "nodes", None),
        check_vma=False,
    )
```

time: 311 us -> 78.4 us (0.25)
  the two profiles are of different devices: /device:TPU:7 before, /device:TPU:1 now
where the time goes in v1:
time: 78.4 us; the launch traced here: 78.2 us
  Pallas kernels  73 us (93%)
  local copies, waits for them, and re-layouts  5.23 us (7%)
    pallas_call x1, Pallas kernels, per_device(): pl.pallas_call(kernel, out_shape=jax.ShapeDtypeStruct(design.shape, jnp.f...  73 us
    unnamed x11, local copies, waits for them, and re-layouts  5.23 us

profile of v1, /device:TPU:1, one launch (start us, length us, event | category | flops | bytes accessed | tf_op | source)
XLA Modules:
  0.0 78.2 jit_solution(3379100209833281242)
XLA Ops:
  0.0 0.0 copy-start
  0.0 1.9 %copy-done = f32[4,3,4,64,256]{4,3,2,1,0:T(8,128)S(1)} copy-done((f32[4,3,4,64,256]{4,3,2,1,0:T(8,128)S(1)}, f32[4,3,4,64,256]{4,3,2,1,0:T(8,128)}, u32[]{:S(2)}) %copy-start) | copy-done | bytes 3145752
  1.9 0.0 copy-start.1
  1.9 0.8 copy-done.1
  2.6 0.0 copy-start.2
  2.7 0.7 copy-done.2
  3.3 0.0 copy-start.3
  3.3 0.7 copy-done.3
  4.0 0.0 copy-start.4
  4.0 0.7 copy-done.4
  4.6 73.0 %sensitivity.1 = f32[4,8,256]{2,1,0:T(8,128)S(1)} custom-call(f32[4,3,4,64,256]{4,3,2,1,0:T(8,128)S(1)} %copy-done, s32[4]{0:T(128)S(1)} %copy-done.2, f32[25]{0:T(128)S(1)} %copy-done.3, f32[25]{0:T(128)S(1)} %copy-done.4, f32[4,8,256]{2,1,0:T(8,128)S(1)} %copy-done.1), custom_call_target="tpu_custom_call" | custom-call | flops 40000000 | bytes 4000000 | tf_op jit(solution)/shard_map/sensitivity/pallas_call | solution.py:386
  77.6 0.6 copy.7
Async XLA Ops:
  0.0 1.9 %copy-start = (f32[4,3,4,64,256]{4,3,2,1,0:T(8,128)S(1)}, f32[4,3,4,64,256]{4,3,2,1,0:T(8,128)}, u32[]{:S(2)}) copy-start(f32[4,3,4,64,256]{4,3,2,1,0:T(8,128)} %disp.1) | copy-start | bytes 9437188
  1.9 0.8 copy-start.1
  2.6 0.7 copy-start.2
  3.3 0.7 copy-start.3
  4.0 0.7 copy-start.4

commit v2 on v1

--- a/solution.py
+++ b/solution.py
@@ -13,6 +13,9 @@
 ETA = 0.5
 RADIUS = 2.5
 MESH = pl.DeviceIdType.MESH
+RUN = 4
+RELAY_DOWN = {1: (3, 0), 4: (3, 1), 2: (1, 0), 5: (2, 0)}
+RELAY_UP = {1: (0, 0), 4: (0, 1), 2: (2, 1), 5: (1, 1)}
 
 
 def weight(dz, dy, dx):
@@ -95,27 +98,28 @@
     ]
 
 
-def make_kernel(groups, slabs, slots, planes, rows, cols, tile):
+def make_kernel(groups, slabs, nodes, slots, planes, rows, cols, tile):
     half = slots // 2
     chips = groups // 2
     below = planes + 1
 
     def kernel(
-        disp, slot_node, node_weight, node_stiffness, design, out,
-        field, low_face, high_face, sums, sibling, pair, arrived,
+        disp, slot_node_in, node_weight_in, node_stiffness_in, design_in, out,
+        slot_node, node_weight, node_stiffness, design, field, low_face, high_face, sums, sibling, pair, arrived,
         des_edge, des_z, des_y, des_c, fac, fac_low,
         sen, sen_edge, sen_low, sen_high, sen_y, sen_cl, sen_ch, pad,
-        load_sem, send_sem, recv_sem,
+        relay, load_sem, small_sem, send_sem, recv_sem, face_send, face_recv, relay_send, relay_recv,
     ):
         group = lax.axis_index("nodes")
         slab = lax.axis_index("space")
         core = lax.rem(group, 2)
         chip = lax.div(group, 2)
-        down = lax.rem(slab + slabs - 1, slabs)
-        up = lax.rem(slab + 1, slabs)
+        place = lax.rem(slab, RUN)
+        run = slab - place
+        down, up = slab - 1, slab + 1
         has_prev, has_next = group > 0, group < groups - 1
-        slab_low = jnp.where(slab > 0, 1.0, 0.0).astype(jnp.float32)
-        slab_high = jnp.where(slab < slabs - 1, 1.0, 0.0).astype(jnp.float32)
+        has_down, has_up = slab > 0, slab < slabs - 1
+        run_down, run_up = run > 0, run < slabs - RUN
         mate = (group + 1 - 2 * core, slab)
         peers = [(2 * lax.rem(chip + k, chips) + core, slab) for k in range(1, chips)]
 
@@ -125,12 +129,28 @@
             else:
                 pl.when(condition)(action)
 
+        small = []
+        for number, (source, target) in enumerate(
+            (
+                (design_in, design),
+                (slot_node_in, slot_node),
+                (node_weight_in, node_weight),
+                (node_stiffness_in, node_stiffness),
+            )
+        ):
+            small.append(pltpu.make_async_copy(source, target, small_sem.at[number]))
+            small[-1].start()
+
         aside = group + 2 * core - 1
-        partners = [(mate, None), ((group, down), None), ((group, up), None)]
-        partners += [(peer, None) for peer in peers]
+        partners = [(mate, None)] + [(peer, None) for peer in peers]
         partners.append(((aside, slab), (aside >= 0) & (aside < groups)))
+        partners += [((group, run + lax.rem(place + k, RUN)), None) for k in range(1, RUN)]
+        partners += [((group, run - 1), run_down), ((group, run + RUN), run_up)]
+        for k in range(1, RUN):
+            partners.append(((group, slab - 1 - k), run_down & (place == 0)))
+            partners.append(((group, slab + 1 + k), run_up & (place == RUN - 1)))
         for cond, step in ((has_prev, -1), (has_next, 1)):
-            partners += [((group + step, where), cond) for where in (down, up)]
+            partners += [((group + step, down), cond & has_down), ((group + step, up), cond & has_up)]
         barrier = pltpu.get_barrier_semaphore()
         for device, cond in partners:
             when(cond, lambda: pl.semaphore_signal(barrier, inc=1, device_id=device, device_id_type=MESH))
@@ -150,6 +170,15 @@
             for slot in range(half):
                 low_face[slot, comp, rows : rows + 8, :] = zero_rows
                 high_face[slot, comp, rows : rows + 8, :] = zero_rows
+
+        def clear(face_ref):
+            for slot in range(half):
+                for comp in range(3):
+                    face_ref[slot, comp, 0:rows, :] = jnp.zeros((rows, cols), jnp.float32)
+
+        pl.when(slab == 0)(lambda: clear(low_face))
+        pl.when(slab == slabs - 1)(lambda: clear(high_face))
+        small[0].wait()
         des_edge[0] = design[:, 0:2, :]
         des_edge[1] = design[:, tile - 2 : tile, :]
 
@@ -167,13 +196,15 @@
 
         def halo(edge, z_src, z_dst, y_dst, c_dst):
             copies = []
-            for side, where in ((0, down), (1, up)):
-                copies.append((remote(z_src[side], z_dst[side], (group, where)), None, None))
+            ways = ((0, down, has_down, has_up), (1, up, has_up, has_down))
+            for side, where, send_z, recv_z in ways:
+                copies.append((remote(z_src[side], z_dst[side], (group, where)), send_z, recv_z))
             for rim, (step, send_if, recv_if) in enumerate(((-1, has_prev, has_next), (1, has_next, has_prev))):
                 copies.append((remote(edge.at[rim], y_dst.at[rim], (group + step, slab)), send_if, recv_if))
-                for side, where in ((0, down), (1, up)):
+                for side, where, send_z, recv_z in ways:
                     part = edge.at[rim, pl.ds(*((0, edge.shape[1] - 2) if side == 0 else (edge.shape[1] - 2, 2)))]
-                    copies.append((remote(part, c_dst[side].at[rim], (group + step, where)), send_if, recv_if))
+                    copy = remote(part, c_dst[side].at[rim], (group + step, where))
+                    copies.append((copy, send_if & send_z, recv_if & recv_z))
             return copies
 
         def start_all(copies):
@@ -184,6 +215,49 @@
             for copy, send_if, recv_if in copies:
                 when(recv_if, copy.wait_recv)
                 when(send_if, copy.wait_send)
+
+        face_of = lambda faces, plane: faces.at[plane // 3, plane % 3, pl.ds(0, rows), :]
+
+        def face_copy(way, plane, where, stop=None, source=None, sent=None):
+            if source is None:
+                source = (
+                    disp.at[plane // 3, plane % 3, 0]
+                    if way == 0
+                    else disp.at[half + plane // 3, plane % 3, planes - 1]
+                )
+            return pltpu.make_async_remote_copy(
+                src_ref=source,
+                dst_ref=face_of((high_face, low_face)[way], plane) if stop is None else relay.at[stop],
+                send_sem=face_send.at[way, plane] if sent is None else sent,
+                recv_sem=face_recv.at[way, plane] if stop is None else relay_recv.at[stop],
+                device_id=(group, where),
+                device_id_type=MESH,
+            )
+
+        ways = (
+            (0, down, has_down, has_up, RELAY_DOWN, 0, run_down, run - 1),
+            (1, up, has_up, has_down, RELAY_UP, RUN - 1, run_up, run + RUN),
+        )
+        for plane in (1, 2, 5, 4, 0, 3):
+            for way, where, send_if, _, relays, end, crosses, _ in ways:
+                if plane in relays:
+                    at, stop = relays[plane]
+                    pl.when(crosses & (place == end))(face_copy(way, plane, run + at, stop).start)
+                    pl.when(place != end)(face_copy(way, plane, where).start)
+                else:
+                    pl.when(send_if)(face_copy(way, plane, where).start)
+
+        def pass_on(stop):
+            for way, _, _, _, relays, _, crosses, target in ways:
+                for plane, (at, slot) in relays.items():
+                    if slot == stop:
+
+                        def forward():
+                            copy = face_copy(way, plane, target, source=relay.at[stop], sent=relay_send.at[stop])
+                            face_copy(way, plane, target, stop).wait_recv()
+                            copy.start()
+
+                        pl.when(crosses & (place == at))(forward)
 
         design_halo = halo(
             des_edge,
@@ -193,18 +267,8 @@
             (des_c.at[1], des_c.at[0]),
         )
         start_all(design_halo)
-        to_down, to_up = [], []
-        for slot in range(half):
-            to_down.append(
-                remote(disp.at[slot, :, 0], high_face.at[slot, :, pl.ds(0, rows), :], (group, down))
-            )
-            to_down[-1].start()
-            to_up.append(
-                remote(
-                    disp.at[half + slot, :, planes - 1], low_face.at[slot, :, pl.ds(0, rows), :], (group, up)
-                )
-            )
-            to_up[-1].start()
+        for copy in small[1:]:
+            copy.wait()
 
         coef = []
         for slot in range(slots):
@@ -216,12 +280,9 @@
         last = lax.broadcasted_iota(jnp.int32, (8, cols), 1) == cols - 1
         next_rows = lax.broadcasted_iota(jnp.int32, (8, cols), 0) == 0
 
-        def modes_of(plane_ref, block, gain=None):
+        def modes_of(plane_ref, block):
             def load(comp):
-                pair_of = [
-                    plane_ref[comp, pl.ds(pl.multiple_of((block + k) * 8, 8), 8), :] for k in range(2)
-                ]
-                return pair_of if gain is None else [v * gain for v in pair_of]
+                return [plane_ref[comp, pl.ds(pl.multiple_of((block + k) * 8, 8), 8), :] for k in range(2)]
 
             return plane_modes(load, next_rows, last)
 
@@ -233,22 +294,23 @@
                 for layer in range(planes - 1):
                     above = modes_of(field.at[slot, :, layer + 1], block)
                     value = coef[slot] * layer_energy(here, above)
-                    place = (lax.rem(block, 2), lax.div(block, 2), layer + 1)
-                    sums[place] = value if slot == 0 else sums[place] + value
+                    where = (lax.rem(block, 2), lax.div(block, 2), layer + 1)
+                    sums[where] = value if slot == 0 else sums[where] + value
                     here = above
                 return carry
 
             lax.fori_loop(0, rows // 8, block_step, 0)
+            if slot < 2:
+                pass_on(slot)
 
         wait_all(design_halo)
         pad[pl.ds(2, planes), pl.ds(8, tile), :] = design[...]
-        pad[pl.ds(0, 2), pl.ds(8, tile), :] = des_z[0] * slab_low
-        pad[pl.ds(planes + 2, 2), pl.ds(8, tile), :] = des_z[1] * slab_high
+        pad[pl.ds(0, 2), pl.ds(8, tile), :] = jnp.where(has_down, des_z[0], 0.0)
+        pad[pl.ds(planes + 2, 2), pl.ds(8, tile), :] = jnp.where(has_up, des_z[1], 0.0)
         for rim, (first, cond) in enumerate(((16, has_next), (6, has_prev))):
-            inside = lambda v: jnp.where(cond, v, 0.0)
-            pad[pl.ds(2, planes), pl.ds(first, 2), :] = inside(des_y[rim])
-            pad[pl.ds(0, 2), pl.ds(first, 2), :] = inside(des_c[0, rim]) * slab_low
-            pad[pl.ds(planes + 2, 2), pl.ds(first, 2), :] = inside(des_c[1, rim]) * slab_high
+            pad[pl.ds(2, planes), pl.ds(first, 2), :] = jnp.where(cond, des_y[rim], 0.0)
+            pad[pl.ds(0, 2), pl.ds(first, 2), :] = jnp.where(cond & has_down, des_c[0, rim], 0.0)
+            pad[pl.ds(planes + 2, 2), pl.ds(first, 2), :] = jnp.where(cond & has_up, des_c[1, rim], 0.0)
 
         row_at = lax.broadcasted_iota(jnp.int32, (tile, cols), 0) + group * tile
         ones = []
@@ -269,29 +331,41 @@
             slope = BETA * (1.0 - level * level) / scale
             fac[plane] = (-3.0 * (1.0 - E_FLOOR)) * (projected * projected) * slope / cover
         factor_up = remote(fac.at[planes - 1], fac_low, (group, up))
-        factor_up.start()
+        pl.when(has_up)(factor_up.start)
 
         for slot in range(half):
-            to_up[slot].wait_recv()
-            to_down[slot].wait_recv()
+            for comp in range(3):
+                for way, where, _, recv_if, *_ in ways:
+                    pl.when(recv_if)(face_copy(way, 3 * slot + comp, where).wait_recv)
 
             def face_step(block, carry):
-                place = lambda layer: (lax.rem(block, 2), lax.div(block, 2), layer)
+                spot = lambda layer: (lax.rem(block, 2), lax.div(block, 2), layer)
                 lower = layer_energy(
-                    modes_of(low_face.at[slot], block),
-                    modes_of(field.at[half + slot, :, 0], block, slab_low),
+                    modes_of(low_face.at[slot], block), modes_of(field.at[half + slot, :, 0], block)
                 )
                 value = coef[half + slot] * lower
-                sums[place(0)] = value if slot == 0 else sums[place(0)] + value
+                sums[spot(0)] = value if slot == 0 else sums[spot(0)] + value
                 upper = layer_energy(
-                    modes_of(field.at[slot, :, planes - 1], block),
-                    modes_of(high_face.at[slot], block, slab_high),
+                    modes_of(field.at[slot, :, planes - 1], block), modes_of(high_face.at[slot], block)
                 )
                 value = coef[slot] * upper
-                sums[place(planes)] = value if slot == 0 else sums[place(planes)] + value
+                sums[spot(planes)] = value if slot == 0 else sums[spot(planes)] + value
                 return carry
 
             lax.fori_loop(0, rows // 8, face_step, 0)
+
+        def top():
+            def top_step(block, carry):
+                spot = (lax.rem(block, 2), lax.div(block, 2), planes)
+                zero = jnp.zeros((8, cols), jnp.float32)
+                for slot in range(half, slots):
+                    modes = modes_of(field.at[slot, :, planes - 1], block)
+                    sums[spot] += coef[slot] * layer_energy(modes, [(zero,) * 4] * 3)
+                return carry
+
+            lax.fori_loop(0, rows // 8, top_step, 0)
+
+        pl.when(slab == slabs - 1)(top)
 
         swap = remote(sums.at[1 - core], sibling, mate)
         swap.start()
@@ -302,12 +376,12 @@
         for k in range(1, chips):
             spread.append(remote(pair.at[lax.rem(chip + k, chips)], arrived.at[k - 1], peers[k - 1]))
             spread[-1].start()
-        factor_up.wait_recv()
+        pl.when(has_down)(factor_up.wait_recv)
         for copy in spread:
             copy.wait_recv()
         for plane in range(below):
             total = pair[chip, plane] + add_up([arrived[k, plane] for k in range(chips - 1)])
-            sen[plane] = total * (fac_low[...] if plane == 0 else fac[plane - 1])
+            sen[plane] = total * (jnp.where(has_down, fac_low[...], 0.0) if plane == 0 else fac[plane - 1])
         sen_edge[0] = sen[:, 0:2, :]
         sen_edge[1] = sen[:, tile - 2 : tile, :]
 
@@ -321,32 +395,44 @@
         start_all(sens_halo)
         wait_all(sens_halo)
 
-        def place_rows(first, own, lower, upper):
+        def place_rows(first, cond, own, lower, upper):
             span = pl.ds(first, own.shape[1])
-            pad[0, span, :] = lower[0] * slab_low
-            pad[1, span, :] = (lower[1] + own[0]) * slab_low
+            inside = lambda flag, v: v if flag is None else jnp.where(flag, v, 0.0)
+            both = lambda flag: flag if cond is None else cond & flag
+            pad[0, span, :] = inside(both(has_down), lower[0])
+            pad[1, span, :] = inside(both(has_down), lower[1] + own[0])
             for plane in range(planes - 1):
-                pad[2 + plane, span, :] = own[1 + plane]
-            pad[1 + planes, span, :] = own[planes] + upper[0]
-            pad[2 + planes, span, :] = upper[1] * slab_high
-            pad[3 + planes, span, :] = upper[2] * slab_high
-
-        place_rows(8, sen[...], sen_low[...], sen_high[...])
+                pad[2 + plane, span, :] = inside(cond, own[1 + plane])
+            pad[1 + planes, span, :] = inside(cond, own[planes]) + inside(both(has_up), upper[0])
+            pad[2 + planes, span, :] = inside(both(has_up), upper[1])
+            pad[3 + planes, span, :] = inside(both(has_up), upper[2])
+
+        place_rows(8, None, sen, sen_low, sen_high)
         for rim, (first, cond) in enumerate(((16, has_next), (6, has_prev))):
-            inside = lambda v: jnp.where(cond, v, 0.0)
-            place_rows(first, inside(sen_y[rim]), inside(sen_cl[rim]), inside(sen_ch[rim]))
+            place_rows(first, cond, sen_y.at[rim], sen_cl.at[rim], sen_ch.at[rim])
         sens_rows = [row_sums(pad, p) for p in range(planes + 4)]
         for plane in range(planes):
             out[plane] = smooth(z_sums(sens_rows, plane + 2), cols)
 
         swap.wait_send()
-        factor_up.wait_send()
-        for copy in spread + to_up + to_down:
+        pl.when(has_up)(factor_up.wait_send)
+        for copy in spread:
             copy.wait_send()
+        for plane in range(3 * half):
+            for way, where, send_if, *_ in ways:
+                pl.when(send_if)(face_copy(way, plane, where).wait_send)
+        for way, where, _, _, relays, _, crosses, _ in ways:
+            for plane, (at, stop) in relays.items():
+                copy = face_copy(way, plane, where, source=relay.at[stop], sent=relay_send.at[stop])
+                pl.when(crosses & (place == at))(copy.wait_send)
 
     vmem = lambda *shape: pltpu.VMEM(shape, jnp.float32)
-    copies = 8 + 2 * half + 1 + 1 + (chips - 1) + 8
+    copies = 8 + 1 + 1 + (chips - 1) + 8
     scratch = [
+        pltpu.SMEM((slots,), jnp.int32),
+        pltpu.SMEM((nodes,), jnp.float32),
+        pltpu.SMEM((nodes,), jnp.float32),
+        vmem(planes, tile, cols),
         vmem(slots, 3, planes, rows + 8, cols),
         vmem(half, 3, rows + 8, cols),
         vmem(half, 3, rows + 8, cols),
@@ -368,9 +454,15 @@
         vmem(2, 2, 2, cols),
         vmem(2, 3, 2, cols),
         vmem(planes + 4, 24, cols),
+        vmem(2, rows, cols),
         pltpu.SemaphoreType.DMA((slots,)),
+        pltpu.SemaphoreType.DMA((4,)),
         pltpu.SemaphoreType.DMA((copies,)),
         pltpu.SemaphoreType.DMA((copies,)),
+        pltpu.SemaphoreType.DMA((2, 3 * half)),
+        pltpu.SemaphoreType.DMA((2, 3 * half)),
+        pltpu.SemaphoreType.DMA((2,)),
+        pltpu.SemaphoreType.DMA((2,)),
     ]
     return kernel, scratch
 
@@ -380,17 +472,15 @@
 
     def per_device(displacement, slot_node, node_weight, node_stiffness, design):
         slots, _, planes, rows, cols = displacement.shape
-        kernel, scratch = make_kernel(groups, slabs, slots, planes, rows, cols, design.shape[1])
-        smem = pl.BlockSpec(memory_space=pltpu.SMEM)
-        vmem = pl.BlockSpec(memory_space=pltpu.VMEM)
+        kernel, scratch = make_kernel(groups, slabs, node_weight.shape[0], slots, planes, rows, cols, design.shape[1])
         return pl.pallas_call(
             kernel,
             out_shape=jax.ShapeDtypeStruct(design.shape, jnp.float32),
-            in_specs=[pl.BlockSpec(memory_space=pl.ANY), smem, smem, smem, vmem],
-            out_specs=vmem,
+            in_specs=[pl.BlockSpec(memory_space=pltpu.HBM)] * 5,
+            out_specs=pl.BlockSpec(memory_space=pltpu.VMEM),
             scratch_shapes=scratch,
             compiler_params=pltpu.CompilerParams(
-                collective_id=0, has_side_effects=True, vmem_limit_bytes=48 * 2**20
+                collective_id=0, has_side_effects=True, vmem_limit_bytes=60 * 2**20
             ),
             cost_estimate=pl.CostEstimate(flops=40_000_000, bytes_accessed=4_000_000, transcendentals=8192),
             name="sensitivity",

time: 78.4 us -> 51.9 us (0.66)
  the two profiles are of different devices: /device:TPU:1 before, /device:TPU:31 now
where the time goes in v2:
time: 51.9 us; the launch traced here: 51.8 us
  Pallas kernels  50.4 us (97%)
  local copies, waits for them, and re-layouts  1.38 us (3%)
    pallas_call x1, Pallas kernels, per_device(): pl.pallas_call(kernel, out_shape=jax.ShapeDtypeStruct(design.shape, jnp.f...  50.4 us
    unnamed x1, local copies, waits for them, and re-layouts  1.38 us

profile of v2, /device:TPU:31, one launch (start us, length us, event | category | flops | bytes accessed | tf_op | source)
XLA Modules:
  0.0 51.8 jit_solution(10707535705947979751)
XLA Ops:
  0.0 50.4 %sensitivity.1 = f32[4,8,256]{2,1,0:T(8,128)} custom-call(f32[4,3,4,64,256]{4,3,2,1,0:T(8,128)} %disp.1, s32[4]{0:T(128)} %slot_node_in.1, f32[25]{0:T(128)} %node_weight_in.1, f32[25]{0:T(128)} %node_stiffness_in.1, f32[4,8,256]{2,1,0:T(8,128)} %design_in.1), custom_call_target="tpu_custom_call" | custom-call | flops 40000000 | bytes 4000000 | tf_op jit(solution)/shard_map/sensitivity/pallas_call | solution.py:476
  50.4 1.4 %copy.7 = f32[4,8,256]{2,1,0:T(8,128)} copy(f32[4,8,256]{2,1,0:T(8,128)} %sensitivity.1) | data formatting | bytes 65536

commit v3 on v2

--- a/solution.py
+++ b/solution.py
@@ -101,14 +101,14 @@
 def make_kernel(groups, slabs, nodes, slots, planes, rows, cols, tile):
     half = slots // 2
     chips = groups // 2
-    below = planes + 1
 
     def kernel(
         disp, slot_node_in, node_weight_in, node_stiffness_in, design_in, out,
-        slot_node, node_weight, node_stiffness, design, field, low_face, high_face, sums, sibling, pair, arrived,
-        des_edge, des_z, des_y, des_c, fac, fac_low,
-        sen, sen_edge, sen_low, sen_high, sen_y, sen_cl, sen_ch, pad,
-        relay, load_sem, small_sem, send_sem, recv_sem, face_send, face_recv, relay_send, relay_recv,
+        slot_node, node_weight, node_stiffness, design, field, low_face, high_face, relay,
+        des_pad, des_z, des_edge, des_y, fac, fac_low,
+        in_sums, in_mate, in_pair, in_peers, sen, sen_pad, sen_low, sen_high, sen_cl, sen_ch, sen_edge, sen_y,
+        face_sums, face_mate, face_pair, face_peers, late, late_z, late_c,
+        load_sem, small_sem, send_sem, recv_sem, face_send, face_recv, relay_send, relay_recv,
     ):
         group = lax.axis_index("nodes")
         slab = lax.axis_index("space")
@@ -129,6 +129,22 @@
             else:
                 pl.when(condition)(action)
 
+        aside = group + 2 * core - 1
+        partners = [(mate, None)] + [(peer, None) for peer in peers]
+        partners.append(((aside, slab), (aside >= 0) & (aside < groups)))
+        partners += [((group, run + lax.rem(place + k, RUN)), None) for k in range(1, RUN)]
+        partners.append(((group, down), run_down & (place == 0)))
+        partners.append(((group, up), run_up & (place == RUN - 1)))
+        barrier = pltpu.get_barrier_semaphore()
+        for device, cond in partners:
+            when(cond, lambda: pl.semaphore_signal(barrier, inc=1, device_id=device, device_id_type=MESH))
+        loads = []
+        for slot in range(slots):
+            load = pltpu.make_async_copy(
+                disp.at[slot], field.at[slot, :, :, pl.ds(0, rows), :], load_sem.at[slot]
+            )
+            load.start()
+            loads.append(load)
         small = []
         for number, (source, target) in enumerate(
             (
@@ -140,81 +156,44 @@
         ):
             small.append(pltpu.make_async_copy(source, target, small_sem.at[number]))
             small[-1].start()
-
-        aside = group + 2 * core - 1
-        partners = [(mate, None)] + [(peer, None) for peer in peers]
-        partners.append(((aside, slab), (aside >= 0) & (aside < groups)))
-        partners += [((group, run + lax.rem(place + k, RUN)), None) for k in range(1, RUN)]
-        partners += [((group, run - 1), run_down), ((group, run + RUN), run_up)]
-        for k in range(1, RUN):
-            partners.append(((group, slab - 1 - k), run_down & (place == 0)))
-            partners.append(((group, slab + 1 + k), run_up & (place == RUN - 1)))
-        for cond, step in ((has_prev, -1), (has_next, 1)):
-            partners += [((group + step, down), cond & has_down), ((group + step, up), cond & has_up)]
-        barrier = pltpu.get_barrier_semaphore()
-        for device, cond in partners:
-            when(cond, lambda: pl.semaphore_signal(barrier, inc=1, device_id=device, device_id_type=MESH))
-
-        loads = []
-        for slot in range(slots):
-            load = pltpu.make_async_copy(
-                disp.at[slot], field.at[slot, :, :, pl.ds(0, rows), :], load_sem.at[slot]
-            )
-            load.start()
-            loads.append(load)
-        zero_rows = jnp.zeros((8, cols), jnp.float32)
-        for comp in range(3):
-            for slot in range(slots):
-                for plane in range(planes):
-                    field[slot, comp, plane, rows : rows + 8, :] = zero_rows
-            for slot in range(half):
-                low_face[slot, comp, rows : rows + 8, :] = zero_rows
-                high_face[slot, comp, rows : rows + 8, :] = zero_rows
-
-        def clear(face_ref):
-            for slot in range(half):
-                for comp in range(3):
-                    face_ref[slot, comp, 0:rows, :] = jnp.zeros((rows, cols), jnp.float32)
-
-        pl.when(slab == 0)(lambda: clear(low_face))
-        pl.when(slab == slabs - 1)(lambda: clear(high_face))
-        small[0].wait()
-        des_edge[0] = design[:, 0:2, :]
-        des_edge[1] = design[:, tile - 2 : tile, :]
-
         pl.semaphore_wait(barrier, sum(1 if cond is None else cond.astype(jnp.int32) for _, cond in partners))
 
-        count = [0]
-
-        def remote(src, dst, device):
-            number = count[0]
-            count[0] += 1
-            return pltpu.make_async_remote_copy(
+        started = []
+
+        def remote(src, dst, device, send_if=None, recv_if=None):
+            number = len(started)
+            copy = pltpu.make_async_remote_copy(
                 src_ref=src, dst_ref=dst, send_sem=send_sem.at[number], recv_sem=recv_sem.at[number],
                 device_id=device, device_id_type=MESH,
             )
-
-        def halo(edge, z_src, z_dst, y_dst, c_dst):
-            copies = []
-            ways = ((0, down, has_down, has_up), (1, up, has_up, has_down))
-            for side, where, send_z, recv_z in ways:
-                copies.append((remote(z_src[side], z_dst[side], (group, where)), send_z, recv_z))
-            for rim, (step, send_if, recv_if) in enumerate(((-1, has_prev, has_next), (1, has_next, has_prev))):
-                copies.append((remote(edge.at[rim], y_dst.at[rim], (group + step, slab)), send_if, recv_if))
-                for side, where, send_z, recv_z in ways:
-                    part = edge.at[rim, pl.ds(*((0, edge.shape[1] - 2) if side == 0 else (edge.shape[1] - 2, 2)))]
-                    copy = remote(part, c_dst[side].at[rim], (group + step, where))
-                    copies.append((copy, send_if & send_z, recv_if & recv_z))
-            return copies
-
-        def start_all(copies):
-            for copy, send_if, _ in copies:
-                when(send_if, copy.start)
-
-        def wait_all(copies):
-            for copy, send_if, recv_if in copies:
+            started.append((copy, send_if, recv_if))
+            when(send_if, copy.start)
+            return started[-1:]
+
+        def arrive(copies):
+            for copy, _, recv_if in copies:
                 when(recv_if, copy.wait_recv)
-                when(send_if, copy.wait_send)
+
+        def send_z(below_src, below_dst, above_src, above_dst):
+            return remote(below_src, below_dst, (group, down), has_down, has_up) + remote(
+                above_src, above_dst, (group, up), has_up, has_down
+            )
+
+        def send_rows(edge, dst):
+            return remote(edge.at[0], dst.at[0], (group - 1, slab), has_prev, has_next) + remote(
+                edge.at[1], dst.at[1], (group + 1, slab), has_next, has_prev
+            )
+
+        rims = ((0, 16, has_next), (1, 6, has_prev))
+        own = pl.ds(8, tile)
+        cut_edges = lambda edge, at, pad_ref, plane: (
+            edge.__setitem__((0, at), pad_ref[plane, 8:10, :]),
+            edge.__setitem__((1, at), pad_ref[plane, tile + 6 : tile + 8, :]),
+        )
+
+        des_planes = send_z(
+            design_in.at[pl.ds(0, 2)], des_z.at[1], design_in.at[pl.ds(planes - 2, 2)], des_z.at[0]
+        )
 
         face_of = lambda faces, plane: faces.at[plane // 3, plane % 3, pl.ds(0, rows), :]
 
@@ -259,16 +238,25 @@
 
                         pl.when(crosses & (place == at))(forward)
 
-        design_halo = halo(
-            des_edge,
-            (design.at[pl.ds(0, 2)], design.at[pl.ds(planes - 2, 2)]),
-            (des_z.at[1], des_z.at[0]),
-            des_y,
-            (des_c.at[1], des_c.at[0]),
-        )
-        start_all(design_halo)
-        for copy in small[1:]:
+        for copy in small:
             copy.wait()
+
+        zero_rows = jnp.zeros((8, cols), jnp.float32)
+        for comp in range(3):
+            for slot in range(slots):
+                for plane in range(planes):
+                    field[slot, comp, plane, rows : rows + 8, :] = zero_rows
+            for slot in range(half):
+                low_face[slot, comp, rows : rows + 8, :] = zero_rows
+                high_face[slot, comp, rows : rows + 8, :] = zero_rows
+
+        def clear(face_ref):
+            for slot in range(half):
+                for comp in range(3):
+                    face_ref[slot, comp, 0:rows, :] = jnp.zeros((rows, cols), jnp.float32)
+
+        pl.when(slab == 0)(lambda: clear(low_face))
+        pl.when(slab == slabs - 1)(lambda: clear(high_face))
 
         coef = []
         for slot in range(slots):
@@ -294,24 +282,42 @@
                 for layer in range(planes - 1):
                     above = modes_of(field.at[slot, :, layer + 1], block)
                     value = coef[slot] * layer_energy(here, above)
-                    where = (lax.rem(block, 2), lax.div(block, 2), layer + 1)
-                    sums[where] = value if slot == 0 else sums[where] + value
+                    spot = (lax.rem(block, 2), lax.div(block, 2), layer)
+                    in_sums[spot] = value if slot == 0 else in_sums[spot] + value
                     here = above
                 return carry
 
             lax.fori_loop(0, rows // 8, block_step, 0)
             if slot < 2:
                 pass_on(slot)
-
-        wait_all(design_halo)
-        pad[pl.ds(2, planes), pl.ds(8, tile), :] = design[...]
-        pad[pl.ds(0, 2), pl.ds(8, tile), :] = jnp.where(has_down, des_z[0], 0.0)
-        pad[pl.ds(planes + 2, 2), pl.ds(8, tile), :] = jnp.where(has_up, des_z[1], 0.0)
-        for rim, (first, cond) in enumerate(((16, has_next), (6, has_prev))):
-            pad[pl.ds(2, planes), pl.ds(first, 2), :] = jnp.where(cond, des_y[rim], 0.0)
-            pad[pl.ds(0, 2), pl.ds(first, 2), :] = jnp.where(cond & has_down, des_c[0, rim], 0.0)
-            pad[pl.ds(planes + 2, 2), pl.ds(first, 2), :] = jnp.where(cond & has_up, des_c[1, rim], 0.0)
-
+            if slot == 1:
+                arrive(des_planes)
+                des_pad[pl.ds(2, planes), own, :] = design[...]
+                des_pad[pl.ds(0, 2), own, :] = jnp.where(has_down, des_z[0], 0.0)
+                des_pad[pl.ds(planes + 2, 2), own, :] = jnp.where(has_up, des_z[1], 0.0)
+                for plane in range(planes + 4):
+                    cut_edges(des_edge, plane, des_pad, plane)
+                des_rows = send_rows(des_edge, des_y)
+
+        def swap(sums, mate_sums):
+            return remote(sums.at[1 - core], mate_sums, mate)
+
+        def spread(sums, mate_sums, pair, peer_sums):
+            for index in range(chips):
+                pair[index] = sums[core, index] + mate_sums[index]
+            copies = []
+            for k in range(1, chips):
+                copies += remote(pair.at[lax.rem(chip + k, chips)], peer_sums.at[k - 1], peers[k - 1])
+            return copies
+
+        def total(pair, peer_sums, layer):
+            return pair[chip, layer] + add_up([peer_sums[k, layer] for k in range(chips - 1)])
+
+        in_swap = swap(in_sums, in_mate)
+
+        arrive(des_rows)
+        for rim, first, cond in rims:
+            des_pad[:, pl.ds(first, 2), :] = jnp.where(cond, des_y[rim], 0.0)
         row_at = lax.broadcasted_iota(jnp.int32, (tile, cols), 0) + group * tile
         ones = []
         for dy in range(3):
@@ -319,7 +325,7 @@
             ones.append(within(row_at) if dy == 0 else within(row_at - dy) + within(row_at + dy))
         base = math.tanh(BETA * ETA)
         scale = base + math.tanh(BETA * (1.0 - ETA))
-        filt_rows = [row_sums(pad, p) for p in range(planes + 4)]
+        filt_rows = [row_sums(des_pad, p) for p in range(planes + 4)]
         for plane in range(planes):
             z = slab * planes + plane
             here = lambda d: jnp.where((z + d >= 0) & (z + d < slabs * planes), 1.0, 0.0)
@@ -330,10 +336,11 @@
             projected = (base + level) / scale
             slope = BETA * (1.0 - level * level) / scale
             fac[plane] = (-3.0 * (1.0 - E_FLOOR)) * (projected * projected) * slope / cover
-        factor_up = remote(fac.at[planes - 1], fac_low, (group, up))
-        pl.when(has_up)(factor_up.start)
-
-        for slot in range(half):
+        factor = remote(fac.at[planes - 1], fac_low, (group, up), has_up, has_down)
+        arrive(in_swap)
+        in_spread = spread(in_sums, in_mate, in_pair, in_peers)
+
+        def face_energy(slot):
             for comp in range(3):
                 for way, where, _, recv_if, *_ in ways:
                     pl.when(recv_if)(face_copy(way, 3 * slot + comp, where).wait_recv)
@@ -344,80 +351,91 @@
                     modes_of(low_face.at[slot], block), modes_of(field.at[half + slot, :, 0], block)
                 )
                 value = coef[half + slot] * lower
-                sums[spot(0)] = value if slot == 0 else sums[spot(0)] + value
+                face_sums[spot(0)] = value if slot == 0 else face_sums[spot(0)] + value
                 upper = layer_energy(
                     modes_of(field.at[slot, :, planes - 1], block), modes_of(high_face.at[slot], block)
                 )
                 value = coef[slot] * upper
-                sums[spot(planes)] = value if slot == 0 else sums[spot(planes)] + value
+                face_sums[spot(1)] = value if slot == 0 else face_sums[spot(1)] + value
                 return carry
 
             lax.fori_loop(0, rows // 8, face_step, 0)
 
-        def top():
+        def top_energy():
             def top_step(block, carry):
-                spot = (lax.rem(block, 2), lax.div(block, 2), planes)
+                spot = (lax.rem(block, 2), lax.div(block, 2), 1)
                 zero = jnp.zeros((8, cols), jnp.float32)
                 for slot in range(half, slots):
                     modes = modes_of(field.at[slot, :, planes - 1], block)
-                    sums[spot] += coef[slot] * layer_energy(modes, [(zero,) * 4] * 3)
+                    face_sums[spot] += coef[slot] * layer_energy(modes, [(zero,) * 4] * 3)
                 return carry
 
             lax.fori_loop(0, rows // 8, top_step, 0)
 
-        pl.when(slab == slabs - 1)(top)
-
-        swap = remote(sums.at[1 - core], sibling, mate)
-        swap.start()
-        swap.wait_recv()
-        for index in range(chips):
-            pair[index] = sums[core, index] + sibling[index]
-        spread = []
-        for k in range(1, chips):
-            spread.append(remote(pair.at[lax.rem(chip + k, chips)], arrived.at[k - 1], peers[k - 1]))
-            spread[-1].start()
-        pl.when(has_down)(factor_up.wait_recv)
-        for copy in spread:
-            copy.wait_recv()
-        for plane in range(below):
-            total = pair[chip, plane] + add_up([arrived[k, plane] for k in range(chips - 1)])
-            sen[plane] = total * (jnp.where(has_down, fac_low[...], 0.0) if plane == 0 else fac[plane - 1])
-        sen_edge[0] = sen[:, 0:2, :]
-        sen_edge[1] = sen[:, tile - 2 : tile, :]
-
-        sens_halo = halo(
-            sen_edge,
-            (sen.at[pl.ds(0, 3)], sen.at[pl.ds(below - 2, 2)]),
-            (sen_high, sen_low),
-            sen_y,
-            (sen_ch, sen_cl),
-        )
-        start_all(sens_halo)
-        wait_all(sens_halo)
-
-        def place_rows(first, cond, own, lower, upper):
-            span = pl.ds(first, own.shape[1])
-            inside = lambda flag, v: v if flag is None else jnp.where(flag, v, 0.0)
-            both = lambda flag: flag if cond is None else cond & flag
-            pad[0, span, :] = inside(both(has_down), lower[0])
-            pad[1, span, :] = inside(both(has_down), lower[1] + own[0])
-            for plane in range(planes - 1):
-                pad[2 + plane, span, :] = inside(cond, own[1 + plane])
-            pad[1 + planes, span, :] = inside(cond, own[planes]) + inside(both(has_up), upper[0])
-            pad[2 + planes, span, :] = inside(both(has_up), upper[1])
-            pad[3 + planes, span, :] = inside(both(has_up), upper[2])
-
-        place_rows(8, None, sen, sen_low, sen_high)
-        for rim, (first, cond) in enumerate(((16, has_next), (6, has_prev))):
-            place_rows(first, cond, sen_y.at[rim], sen_cl.at[rim], sen_ch.at[rim])
-        sens_rows = [row_sums(pad, p) for p in range(planes + 4)]
+        face_energy(0)
+        pl.when(slab == slabs - 1)(top_energy)
+
+        for slot in range(1, half):
+            face_energy(slot)
+        face_swap = swap(face_sums, face_mate)
+
+        def corners(edge, lower, upper, dst):
+            copies = []
+            for rim, step, send_if, recv_if in ((0, -1, has_prev, has_next), (1, 1, has_next, has_prev)):
+                for part, side, where, send_s, recv_s in (
+                    (lower, 1, down, has_down, has_up),
+                    (upper, 0, up, has_up, has_down),
+                ):
+                    copies += remote(
+                        edge.at[rim, part], dst[side].at[rim], (group + step, where), send_if & send_s, recv_if & recv_s
+                    )
+            return copies
+
+        arrive(in_spread)
+        inner = planes - 1
+        for layer in range(inner):
+            sen[layer] = total(in_pair, in_peers, layer) * fac[layer]
+        sen_edge[0, 0:inner] = sen[:, 0:2, :]
+        sen_edge[1, 0:inner] = sen[:, tile - 2 : tile, :]
+        halo = send_z(sen.at[pl.ds(0, 2)], sen_high, sen.at[inner - 1], sen_low)
+        halo += corners(sen_edge, pl.ds(0, 2), inner - 1, (sen_cl, sen_ch))
+
+        arrive(face_swap)
+        face_spread = spread(face_sums, face_mate, face_pair, face_peers)
+        sen_pad[pl.ds(2, inner), own, :] = sen[...]
+        arrive(factor)
+        arrive(face_spread)
+        late[0] = total(face_pair, face_peers, 0) * jnp.where(has_down, fac_low[...], 0.0)
+        late[1] = total(face_pair, face_peers, 1) * fac[inner]
+        late_halo = send_z(late.at[0], late_z.at[1], late.at[1], late_z.at[0])
+        sen_edge[0, inner : inner + 2] = late[:, 0:2, :]
+        sen_edge[1, inner : inner + 2] = late[:, tile - 2 : tile, :]
+        late_halo += corners(sen_edge, inner, inner + 1, (late_c.at[0], late_c.at[1]))
+        late_halo += send_rows(sen_edge, sen_y)
+
+        arrive(halo)
+        sen_pad[0, own, :] = jnp.where(has_down, sen_low[...], 0.0)
+        sen_pad[pl.ds(planes + 2, 2), own, :] = jnp.where(has_up, sen_high[...], 0.0)
+        for rim, first, cond in rims:
+            span = pl.ds(first, 2)
+            sen_pad[0, span, :] = jnp.where(cond & has_down, sen_cl[rim], 0.0)
+            sen_pad[pl.ds(planes + 2, 2), span, :] = jnp.where(cond & has_up, sen_ch[rim], 0.0)
+        arrive(late_halo)
+        sen_pad[1, own, :] = jnp.where(has_down, late[0] + late_z[0], 0.0)
+        sen_pad[planes + 1, own, :] = late[1] + jnp.where(has_up, late_z[1], 0.0)
+        for rim, first, cond in rims:
+            span = pl.ds(first, 2)
+            sen_pad[1, span, :] = jnp.where(cond & has_down, sen_y[rim, inner] + late_c[0, rim], 0.0)
+            sen_pad[pl.ds(2, inner), span, :] = jnp.where(cond, sen_y[rim, 0:inner], 0.0)
+            sen_pad[planes + 1, span, :] = jnp.where(cond, sen_y[rim, inner + 1], 0.0) + jnp.where(
+                cond & has_up, late_c[1, rim], 0.0
+            )
+        sens_rows = [row_sums(sen_pad, p) for p in range(planes + 4)]
         for plane in range(planes):
             out[plane] = smooth(z_sums(sens_rows, plane + 2), cols)
 
-        swap.wait_send()
-        pl.when(has_up)(factor_up.wait_send)
-        for copy in spread:
-            copy.wait_send()
+        for copy, send_if, _ in started:
+            when(send_if, copy.wait_send)
         for plane in range(3 * half):
             for way, where, send_if, *_ in ways:
                 pl.when(send_if)(face_copy(way, plane, where).wait_send)
@@ -427,7 +445,8 @@
                 pl.when(crosses & (place == at))(copy.wait_send)
 
     vmem = lambda *shape: pltpu.VMEM(shape, jnp.float32)
-    copies = 8 + 1 + 1 + (chips - 1) + 8
+    copies = 2 + 2 + 1 + 2 * chips + 6 + 8
+    inner = planes - 1
     scratch = [
         pltpu.SMEM((slots,), jnp.int32),
         pltpu.SMEM((nodes,), jnp.float32),
@@ -436,25 +455,32 @@
         vmem(slots, 3, planes, rows + 8, cols),
         vmem(half, 3, rows + 8, cols),
         vmem(half, 3, rows + 8, cols),
-        vmem(2, chips, below, tile, cols),
-        vmem(chips, below, tile, cols),
-        vmem(chips, below, tile, cols),
-        vmem(chips - 1, below, tile, cols),
-        vmem(2, planes, 2, cols),
+        vmem(2, rows, cols),
+        vmem(planes + 4, 24, cols),
         vmem(2, 2, tile, cols),
-        vmem(2, planes, 2, cols),
-        vmem(2, 2, 2, 2, cols),
+        vmem(2, planes + 4, 2, cols),
+        vmem(2, planes + 4, 2, cols),
         vmem(planes, tile, cols),
         vmem(tile, cols),
-        vmem(below, tile, cols),
-        vmem(2, below, 2, cols),
+        vmem(2, chips, inner, tile, cols),
+        vmem(chips, inner, tile, cols),
+        vmem(chips, inner, tile, cols),
+        vmem(chips - 1, inner, tile, cols),
+        vmem(inner, tile, cols),
+        vmem(planes + 4, 24, cols),
+        vmem(tile, cols),
         vmem(2, tile, cols),
-        vmem(3, tile, cols),
-        vmem(2, below, 2, cols),
+        vmem(2, 2, cols),
         vmem(2, 2, 2, cols),
-        vmem(2, 3, 2, cols),
-        vmem(planes + 4, 24, cols),
-        vmem(2, rows, cols),
+        vmem(2, planes + 1, 2, cols),
+        vmem(2, planes + 1, 2, cols),
+        vmem(2, chips, 2, tile, cols),
+        vmem(chips, 2, tile, cols),
+        vmem(chips, 2, tile, cols),
+        vmem(chips - 1, 2, tile, cols),
+        vmem(2, tile, cols),
+        vmem(2, tile, cols),
+        vmem(2, 2, 2, cols),
         pltpu.SemaphoreType.DMA((slots,)),
         pltpu.SemaphoreType.DMA((4,)),
         pltpu.SemaphoreType.DMA((copies,)),

time: 51.9 us -> 49 us (0.944)
  Pallas kernels: 50.4 us -> 47.5 us
    pallas_call x1, Pallas kernels: 50.4 us -> 47.5 us  [per_device(): pl.pallas_call(kernel, out_shape=jax.ShapeDtypeStruct(design.shape, jnp.f...]
where the time goes in v3:
time: 49 us; the launch traced here: 48.9 us
  Pallas kernels  47.5 us (97%)
  local copies, waits for them, and re-layouts  1.38 us (3%)
    pallas_call x1, Pallas kernels, per_device(): pl.pallas_call(kernel, out_shape=jax.ShapeDtypeStruct(design.shape, jnp.f...  47.5 us
    unnamed x1, local copies, waits for them, and re-layouts  1.38 us

profile of v3, /device:TPU:31, one launch (start us, length us, event | category | flops | bytes accessed | tf_op | source)
XLA Modules:
  0.0 48.9 jit_solution(11250979324116024984)
XLA Ops:
  0.0 47.5 %sensitivity.1 = f32[4,8,256]{2,1,0:T(8,128)} custom-call(f32[4,3,4,64,256]{4,3,2,1,0:T(8,128)} %disp.1, s32[4]{0:T(128)} %slot_node_in.1, f32[25]{0:T(128)} %node_weight_in.1, f32[25]{0:T(128)} %node_stiffness_in.1, f32[4,8,256]{2,1,0:T(8,128)} %design_in.1), custom_call_target="tpu_custom_call" | custom-call | flops 40000000 | bytes 4000000 | tf_op jit(solution)/shard_map/sensitivity/pallas_call | solution.py:502
  47.5 1.4 %copy.7 = f32[4,8,256]{2,1,0:T(8,128)} copy(f32[4,8,256]{2,1,0:T(8,128)} %sensitivity.1) | data formatting | bytes 65536

commit v4 on v3

--- a/solution.py
+++ b/solution.py
@@ -104,7 +104,7 @@
 
     def kernel(
         disp, slot_node_in, node_weight_in, node_stiffness_in, design_in, out,
-        slot_node, node_weight, node_stiffness, design, field, low_face, high_face, relay,
+        slot_node, node_weight, node_stiffness, design, field, kept, low_face, high_face, relay,
         des_pad, des_z, des_edge, des_y, fac, fac_low,
         in_sums, in_mate, in_pair, in_peers, sen, sen_pad, sen_low, sen_high, sen_cl, sen_ch, sen_edge, sen_y,
         face_sums, face_mate, face_pair, face_peers, late, late_z, late_c,
@@ -130,11 +130,10 @@
                 pl.when(condition)(action)
 
         aside = group + 2 * core - 1
-        partners = [(mate, None)] + [(peer, None) for peer in peers]
+        partners = [((group, down), run_down & (place == 0)), ((group, up), run_up & (place == RUN - 1))]
+        partners += [((group, run + lax.rem(place + k, RUN)), None) for k in range(1, RUN)]
+        partners += [(mate, None)] + [(peer, None) for peer in peers]
         partners.append(((aside, slab), (aside >= 0) & (aside < groups)))
-        partners += [((group, run + lax.rem(place + k, RUN)), None) for k in range(1, RUN)]
-        partners.append(((group, down), run_down & (place == 0)))
-        partners.append(((group, up), run_up & (place == RUN - 1)))
         barrier = pltpu.get_barrier_semaphore()
         for device, cond in partners:
             when(cond, lambda: pl.semaphore_signal(barrier, inc=1, device_id=device, device_id_type=MESH))
@@ -217,14 +216,17 @@
             (0, down, has_down, has_up, RELAY_DOWN, 0, run_down, run - 1),
             (1, up, has_up, has_down, RELAY_UP, RUN - 1, run_up, run + RUN),
         )
-        for plane in (1, 2, 5, 4, 0, 3):
-            for way, where, send_if, _, relays, end, crosses, _ in ways:
-                if plane in relays:
-                    at, stop = relays[plane]
-                    pl.when(crosses & (place == end))(face_copy(way, plane, run + at, stop).start)
-                    pl.when(place != end)(face_copy(way, plane, where).start)
-                else:
-                    pl.when(send_if)(face_copy(way, plane, where).start)
+        for plane in (0, 1, 2, 5, 4, 3):
+            for way, where, _, _, relays, end, crosses, _ in ways:
+                copy = (
+                    face_copy(way, plane, run + relays[plane][0], relays[plane][1])
+                    if plane in relays
+                    else face_copy(way, plane, where)
+                )
+                pl.when(crosses & (place == end))(copy.start)
+        for plane in range(3 * half):
+            for way, where, _, _, _, end, _, _ in ways:
+                pl.when(place != end)(face_copy(way, plane, where).start)
 
         def pass_on(stop):
             for way, _, _, _, relays, _, crosses, target in ways:
@@ -274,20 +276,33 @@
 
             return plane_modes(load, next_rows, last)
 
+        def keep(slot, block, modes):
+            for comp in range(3):
+                for mode in range(4):
+                    kept[slot, comp, mode, pl.ds(pl.multiple_of(block * 8, 8), 8), :] = modes[comp][mode]
+
+        def kept_modes(slot, block):
+            span = pl.ds(pl.multiple_of(block * 8, 8), 8)
+            return [[kept[slot, comp, mode, span, :] for mode in range(4)] for comp in range(3)]
+
         for slot in range(slots):
             loads[slot].wait()
 
             def block_step(block, carry):
                 here = modes_of(field.at[slot, :, 0], block)
+                if slot >= half:
+                    keep(slot, block, here)
                 for layer in range(planes - 1):
                     above = modes_of(field.at[slot, :, layer + 1], block)
                     value = coef[slot] * layer_energy(here, above)
                     spot = (lax.rem(block, 2), lax.div(block, 2), layer)
                     in_sums[spot] = value if slot == 0 else in_sums[spot] + value
                     here = above
+                if slot < half:
+                    keep(slot, block, here)
                 return carry
 
-            lax.fori_loop(0, rows // 8, block_step, 0)
+            lax.fori_loop(0, rows // 8, block_step, 0, unroll=2)
             if slot < 2:
                 pass_on(slot)
             if slot == 1:
@@ -347,19 +362,15 @@
 
             def face_step(block, carry):
                 spot = lambda layer: (lax.rem(block, 2), lax.div(block, 2), layer)
-                lower = layer_energy(
-                    modes_of(low_face.at[slot], block), modes_of(field.at[half + slot, :, 0], block)
-                )
+                lower = layer_energy(modes_of(low_face.at[slot], block), kept_modes(half + slot, block))
                 value = coef[half + slot] * lower
                 face_sums[spot(0)] = value if slot == 0 else face_sums[spot(0)] + value
-                upper = layer_energy(
-                    modes_of(field.at[slot, :, planes - 1], block), modes_of(high_face.at[slot], block)
-                )
+                upper = layer_energy(kept_modes(slot, block), modes_of(high_face.at[slot], block))
                 value = coef[slot] * upper
                 face_sums[spot(1)] = value if slot == 0 else face_sums[spot(1)] + value
                 return carry
 
-            lax.fori_loop(0, rows // 8, face_step, 0)
+            lax.fori_loop(0, rows // 8, face_step, 0, unroll=4)
 
         def top_energy():
             def top_step(block, carry):
@@ -453,6 +464,7 @@
         pltpu.SMEM((nodes,), jnp.float32),
         vmem(planes, tile, cols),
         vmem(slots, 3, planes, rows + 8, cols),
+        vmem(slots, 3, 4, rows, cols),
         vmem(half, 3, rows + 8, cols),
         vmem(half, 3, rows + 8, cols),
         vmem(2, rows, cols),

time: 49 us -> 46.8 us (0.955)
  the two profiles are of different devices: /device:TPU:31 before, /device:TPU:7 now
where the time goes in v4:
time: 46.8 us; the launch traced here: 46.7 us
  Pallas kernels  45.3 us (97%)
  local copies, waits for them, and re-layouts  1.38 us (3%)
    pallas_call x1, Pallas kernels, per_device(): pl.pallas_call(kernel, out_shape=jax.ShapeDtypeStruct(design.shape, jnp.f...  45.3 us
    unnamed x1, local copies, waits for them, and re-layouts  1.38 us

profile of v4, /device:TPU:7, one launch (start us, length us, event | category | flops | bytes accessed | tf_op | source)
XLA Modules:
  0.0 46.7 jit_solution(9911302367356037767)
XLA Ops:
  0.0 45.3 %sensitivity.1 = f32[4,8,256]{2,1,0:T(8,128)} custom-call(f32[4,3,4,64,256]{4,3,2,1,0:T(8,128)} %disp.1, s32[4]{0:T(128)} %slot_node_in.1, f32[25]{0:T(128)} %node_weight_in.1, f32[25]{0:T(128)} %node_stiffness_in.1, f32[4,8,256]{2,1,0:T(8,128)} %design_in.1), custom_call_target="tpu_custom_call" | custom-call | flops 40000000 | bytes 4000000 | tf_op jit(solution)/shard_map/sensitivity/pallas_call | solution.py:514
  45.3 1.4 %copy.7 = f32[4,8,256]{2,1,0:T(8,128)} copy(f32[4,8,256]{2,1,0:T(8,128)} %sensitivity.1) | data formatting | bytes 65536

commit v5 on v4

--- a/solution.py
+++ b/solution.py
@@ -14,8 +14,18 @@
 RADIUS = 2.5
 MESH = pl.DeviceIdType.MESH
 RUN = 4
-RELAY_DOWN = {1: (3, 0), 4: (3, 1), 2: (1, 0), 5: (2, 0)}
-RELAY_UP = {1: (0, 0), 4: (0, 1), 2: (2, 1), 5: (1, 1)}
+RELAY_DOWN = {(1, 0): 3, (1, 1): 3, (4, 0): 1, (4, 1): 2, (2, 0): 1, (2, 1): 1, (5, 0): 2, (5, 1): 2}
+RELAY_UP = {(1, 0): 0, (1, 1): 0, (4, 0): 0, (4, 1): 1, (2, 0): 2, (2, 1): 2, (5, 0): 1, (5, 1): 1}
+FIRST = ({1, 2, 5}, {1})
+
+
+def relay_slots():
+    used, slots = {}, {}
+    for way, relays in enumerate((RELAY_DOWN, RELAY_UP)):
+        for (plane, part), at in relays.items():
+            slots[way, plane, part] = (at, used.get(at, 0))
+            used[at] = used.get(at, 0) + 1
+    return slots, max(used.values())
 
 
 def weight(dz, dy, dx):
@@ -101,6 +111,7 @@
 def make_kernel(groups, slabs, nodes, slots, planes, rows, cols, tile):
     half = slots // 2
     chips = groups // 2
+    slots_of, stops = relay_slots()
 
     def kernel(
         disp, slot_node_in, node_weight_in, node_stiffness_in, design_in, out,
@@ -194,49 +205,48 @@
             design_in.at[pl.ds(0, 2)], des_z.at[1], design_in.at[pl.ds(planes - 2, 2)], des_z.at[0]
         )
 
-        face_of = lambda faces, plane: faces.at[plane // 3, plane % 3, pl.ds(0, rows), :]
-
-        def face_copy(way, plane, where, stop=None, source=None, sent=None):
-            if source is None:
-                source = (
-                    disp.at[plane // 3, plane % 3, 0]
-                    if way == 0
-                    else disp.at[half + plane // 3, plane % 3, planes - 1]
-                )
+        def face_copy(way, plane, where, part=None, stop=None, passed=None):
+            cut = pl.ds(0, rows) if part is None else pl.ds(part * (rows // 2), rows // 2)
+            if passed is not None:
+                source = relay.at[passed]
+            elif way == 0:
+                source = disp.at[plane // 3, plane % 3, 0, cut]
+            else:
+                source = disp.at[half + plane // 3, plane % 3, planes - 1, cut]
+            faces = (high_face, low_face)[way]
             return pltpu.make_async_remote_copy(
                 src_ref=source,
-                dst_ref=face_of((high_face, low_face)[way], plane) if stop is None else relay.at[stop],
-                send_sem=face_send.at[way, plane] if sent is None else sent,
+                dst_ref=faces.at[plane // 3, plane % 3, cut] if stop is None else relay.at[stop],
+                send_sem=face_send.at[way, plane] if passed is None else relay_send.at[passed],
                 recv_sem=face_recv.at[way, plane] if stop is None else relay_recv.at[stop],
                 device_id=(group, where),
                 device_id_type=MESH,
             )
 
         ways = (
-            (0, down, has_down, has_up, RELAY_DOWN, 0, run_down, run - 1),
-            (1, up, has_up, has_down, RELAY_UP, RUN - 1, run_up, run + RUN),
+            (0, down, has_down, has_up, 0, run_down, run - 1),
+            (1, up, has_up, has_down, RUN - 1, run_up, run + RUN),
         )
         for plane in (0, 1, 2, 5, 4, 3):
-            for way, where, _, _, relays, end, crosses, _ in ways:
-                copy = (
-                    face_copy(way, plane, run + relays[plane][0], relays[plane][1])
-                    if plane in relays
-                    else face_copy(way, plane, where)
-                )
-                pl.when(crosses & (place == end))(copy.start)
+            for way, where, _, _, end, crosses, _ in ways:
+                for part in range(2) if (way, plane, 0) in slots_of else (None,):
+                    if (way, plane, part) in slots_of:
+                        at, stop = slots_of[way, plane, part]
+                        pl.when(crosses & (place == end))(face_copy(way, plane, run + at, part, stop).start)
+                    else:
+                        pl.when(crosses & (place == end))(face_copy(way, plane, where, part).start)
         for plane in range(3 * half):
-            for way, where, _, _, _, end, _, _ in ways:
+            for way, where, _, _, end, _, _ in ways:
                 pl.when(place != end)(face_copy(way, plane, where).start)
 
-        def pass_on(stop):
-            for way, _, _, _, relays, _, crosses, target in ways:
-                for plane, (at, slot) in relays.items():
-                    if slot == stop:
+        def pass_on(turn):
+            for way, _, _, _, _, crosses, target in ways:
+                for (relay_way, plane, part), (at, stop) in slots_of.items():
+                    if relay_way == way and (plane in FIRST[way]) == (turn == 0):
 
                         def forward():
-                            copy = face_copy(way, plane, target, source=relay.at[stop], sent=relay_send.at[stop])
-                            face_copy(way, plane, target, stop).wait_recv()
-                            copy.start()
+                            face_copy(way, plane, target, part, stop).wait_recv()
+                            face_copy(way, plane, target, part, passed=stop).start()
 
                         pl.when(crosses & (place == at))(forward)
 
@@ -305,14 +315,6 @@
             lax.fori_loop(0, rows // 8, block_step, 0, unroll=2)
             if slot < 2:
                 pass_on(slot)
-            if slot == 1:
-                arrive(des_planes)
-                des_pad[pl.ds(2, planes), own, :] = design[...]
-                des_pad[pl.ds(0, 2), own, :] = jnp.where(has_down, des_z[0], 0.0)
-                des_pad[pl.ds(planes + 2, 2), own, :] = jnp.where(has_up, des_z[1], 0.0)
-                for plane in range(planes + 4):
-                    cut_edges(des_edge, plane, des_pad, plane)
-                des_rows = send_rows(des_edge, des_y)
 
         def swap(sums, mate_sums):
             return remote(sums.at[1 - core], mate_sums, mate)
@@ -329,6 +331,14 @@
             return pair[chip, layer] + add_up([peer_sums[k, layer] for k in range(chips - 1)])
 
         in_swap = swap(in_sums, in_mate)
+        arrive(des_planes)
+        des_pad[pl.ds(2, planes), own, :] = design[...]
+        des_pad[pl.ds(0, 2), own, :] = jnp.where(has_down, des_z[0], 0.0)
+        des_pad[pl.ds(planes + 2, 2), own, :] = jnp.where(has_up, des_z[1], 0.0)
+        for plane in range(planes + 4):
+            cut_edges(des_edge, plane, des_pad, plane)
+        des_rows = send_rows(des_edge, des_y)
+
 
         arrive(des_rows)
         for rim, first, cond in rims:
@@ -450,10 +460,10 @@
         for plane in range(3 * half):
             for way, where, send_if, *_ in ways:
                 pl.when(send_if)(face_copy(way, plane, where).wait_send)
-        for way, where, _, _, relays, _, crosses, _ in ways:
-            for plane, (at, stop) in relays.items():
-                copy = face_copy(way, plane, where, source=relay.at[stop], sent=relay_send.at[stop])
-                pl.when(crosses & (place == at))(copy.wait_send)
+        for way, where, _, _, _, crosses, _ in ways:
+            for (relay_way, plane, part), (at, stop) in slots_of.items():
+                if relay_way == way:
+                    pl.when(crosses & (place == at))(face_copy(way, plane, where, part, passed=stop).wait_send)
 
     vmem = lambda *shape: pltpu.VMEM(shape, jnp.float32)
     copies = 2 + 2 + 1 + 2 * chips + 6 + 8
@@ -467,7 +477,7 @@
         vmem(slots, 3, 4, rows, cols),
         vmem(half, 3, rows + 8, cols),
         vmem(half, 3, rows + 8, cols),
-        vmem(2, rows, cols),
+        vmem(stops, rows // 2, cols),
         vmem(planes + 4, 24, cols),
         vmem(2, 2, tile, cols),
         vmem(2, planes + 4, 2, cols),
@@ -499,8 +509,8 @@
         pltpu.SemaphoreType.DMA((copies,)),
         pltpu.SemaphoreType.DMA((2, 3 * half)),
         pltpu.SemaphoreType.DMA((2, 3 * half)),
-        pltpu.SemaphoreType.DMA((2,)),
-        pltpu.SemaphoreType.DMA((2,)),
+        pltpu.SemaphoreType.DMA((stops,)),
+        pltpu.SemaphoreType.DMA((stops,)),
     ]
     return kernel, scratch
 

time: 46.8 us -> 45.9 us (0.981)
  Pallas kernels: 45.3 us -> 44.4 us
    pallas_call x1, Pallas kernels: 45.3 us -> 44.4 us  [per_device(): pl.pallas_call(kernel, out_shape=jax.ShapeDtypeStruct(design.shape, jnp.f...]
where the time goes in v5:
time: 45.9 us; the launch traced here: 45.8 us
  Pallas kernels  44.4 us (97%)
  local copies, waits for them, and re-layouts  1.38 us (3%)
    pallas_call x1, Pallas kernels, per_device(): pl.pallas_call(kernel, out_shape=jax.ShapeDtypeStruct(design.shape, jnp.f...  44.4 us
    unnamed x1, local copies, waits for them, and re-layouts  1.38 us

profile of v5, /device:TPU:7, one launch (start us, length us, event | category | flops | bytes accessed | tf_op | source)
XLA Modules:
  0.0 45.8 jit_solution(7834308730976807731)
XLA Ops:
  0.0 44.4 %sensitivity.1 = f32[4,8,256]{2,1,0:T(8,128)} custom-call(f32[4,3,4,64,256]{4,3,2,1,0:T(8,128)} %disp.1, s32[4]{0:T(128)} %slot_node_in.1, f32[25]{0:T(128)} %node_weight_in.1, f32[25]{0:T(128)} %node_stiffness_in.1, f32[4,8,256]{2,1,0:T(8,128)} %design_in.1), custom_call_target="tpu_custom_call" | custom-call | flops 40000000 | bytes 4000000 | tf_op jit(solution)/shard_map/sensitivity/pallas_call | solution.py:524
  44.4 1.4 %copy.7 = f32[4,8,256]{2,1,0:T(8,128)} copy(f32[4,8,256]{2,1,0:T(8,128)} %sensitivity.1) | data formatting | bytes 65536

commit v6 on v5

--- a/solution.py
+++ b/solution.py
@@ -217,8 +217,18 @@
             return pltpu.make_async_remote_copy(
                 src_ref=source,
                 dst_ref=faces.at[plane // 3, plane % 3, cut] if stop is None else relay.at[stop],
-                send_sem=face_send.at[way, plane] if passed is None else relay_send.at[passed],
-                recv_sem=face_recv.at[way, plane] if stop is None else relay_recv.at[stop],
+                send_sem=face_send.at[way, plane // 3] if passed is None else relay_send.at[passed],
+                recv_sem=face_recv.at[way, plane // 3] if stop is None else relay_recv.at[stop],
+                device_id=(group, where),
+                device_id_type=MESH,
+            )
+
+        def slot_copy(way, slot, where):
+            return pltpu.make_async_remote_copy(
+                src_ref=disp.at[slot, :, 0] if way == 0 else disp.at[half + slot, :, planes - 1],
+                dst_ref=(high_face, low_face)[way].at[slot, :, pl.ds(0, rows)],
+                send_sem=face_send.at[way, slot],
+                recv_sem=face_recv.at[way, slot],
                 device_id=(group, where),
                 device_id_type=MESH,
             )
@@ -235,9 +245,9 @@
                         pl.when(crosses & (place == end))(face_copy(way, plane, run + at, part, stop).start)
                     else:
                         pl.when(crosses & (place == end))(face_copy(way, plane, where, part).start)
-        for plane in range(3 * half):
+        for slot in range(half):
             for way, where, _, _, end, _, _ in ways:
-                pl.when(place != end)(face_copy(way, plane, where).start)
+                pl.when(place != end)(slot_copy(way, slot, where).start)
 
         def pass_on(turn):
             for way, _, _, _, _, crosses, target in ways:
@@ -366,9 +376,8 @@
         in_spread = spread(in_sums, in_mate, in_pair, in_peers)
 
         def face_energy(slot):
-            for comp in range(3):
-                for way, where, _, recv_if, *_ in ways:
-                    pl.when(recv_if)(face_copy(way, 3 * slot + comp, where).wait_recv)
+            for way, where, _, recv_if, *_ in ways:
+                pl.when(recv_if)(slot_copy(way, slot, where).wait_recv)
 
             def face_step(block, carry):
                 spot = lambda layer: (lax.rem(block, 2), lax.div(block, 2), layer)
@@ -457,9 +466,9 @@
 
         for copy, send_if, _ in started:
             when(send_if, copy.wait_send)
-        for plane in range(3 * half):
+        for slot in range(half):
             for way, where, send_if, *_ in ways:
-                pl.when(send_if)(face_copy(way, plane, where).wait_send)
+                pl.when(send_if)(slot_copy(way, slot, where).wait_send)
         for way, where, _, _, _, crosses, _ in ways:
             for (relay_way, plane, part), (at, stop) in slots_of.items():
                 if relay_way == way:
@@ -507,8 +516,8 @@
         pltpu.SemaphoreType.DMA((4,)),
         pltpu.SemaphoreType.DMA((copies,)),
         pltpu.SemaphoreType.DMA((copies,)),
-        pltpu.SemaphoreType.DMA((2, 3 * half)),
-        pltpu.SemaphoreType.DMA((2, 3 * half)),
+        pltpu.SemaphoreType.DMA((2, half)),
+        pltpu.SemaphoreType.DMA((2, half)),
         pltpu.SemaphoreType.DMA((stops,)),
         pltpu.SemaphoreType.DMA((stops,)),
     ]

time: 45.9 us -> 45.8 us (level)
  no operation moved by 1% of the time
where the time goes in v6:
time: 45.8 us; the launch traced here: 45.6 us
  Pallas kernels  44.2 us (97%)
  local copies, waits for them, and re-layouts  1.38 us (3%)
    pallas_call x1, Pallas kernels, per_device(): pl.pallas_call(kernel, out_shape=jax.ShapeDtypeStruct(design.shape, jnp.f...  44.2 us
    unnamed x1, local copies, waits for them, and re-layouts  1.38 us

profile of v6, /device:TPU:7, one launch (start us, length us, event | category | flops | bytes accessed | tf_op | source)
XLA Modules:
  0.0 45.6 jit_solution(6814405160005074257)
XLA Ops:
  0.0 44.2 %sensitivity.1 = f32[4,8,256]{2,1,0:T(8,128)} custom-call(f32[4,3,4,64,256]{4,3,2,1,0:T(8,128)} %disp.1, s32[4]{0:T(128)} %slot_node_in.1, f32[25]{0:T(128)} %node_weight_in.1, f32[25]{0:T(128)} %node_stiffness_in.1, f32[4,8,256]{2,1,0:T(8,128)} %design_in.1), custom_call_target="tpu_custom_call" | custom-call | flops 40000000 | bytes 4000000 | tf_op jit(solution)/shard_map/sensitivity/pallas_call | solution.py:533
  44.2 1.4 %copy.7 = f32[4,8,256]{2,1,0:T(8,128)} copy(f32[4,8,256]{2,1,0:T(8,128)} %sensitivity.1) | data formatting | bytes 65536

commit v7 on v6

--- a/solution.py
+++ b/solution.py
@@ -14,7 +14,7 @@
 RADIUS = 2.5
 MESH = pl.DeviceIdType.MESH
 RUN = 4
-RELAY_DOWN = {(1, 0): 3, (1, 1): 3, (4, 0): 1, (4, 1): 2, (2, 0): 1, (2, 1): 1, (5, 0): 2, (5, 1): 2}
+RELAY_DOWN = {(1, 0): 3, (1, 1): 3, (4, 0): 1, (3, 1): 3, (4, 1): 2, (2, 0): 1, (2, 1): 1, (5, 0): 2, (5, 1): 2}
 RELAY_UP = {(1, 0): 0, (1, 1): 0, (4, 0): 0, (4, 1): 1, (2, 0): 2, (2, 1): 2, (5, 0): 1, (5, 1): 1}
 FIRST = ({1, 2, 5}, {1})
 
@@ -239,7 +239,7 @@
         )
         for plane in (0, 1, 2, 5, 4, 3):
             for way, where, _, _, end, crosses, _ in ways:
-                for part in range(2) if (way, plane, 0) in slots_of else (None,):
+                for part in range(2) if any((way, plane, k) in slots_of for k in range(2)) else (None,):
                     if (way, plane, part) in slots_of:
                         at, stop = slots_of[way, plane, part]
                         pl.when(crosses & (place == end))(face_copy(way, plane, run + at, part, stop).start)

time: 45.8 us -> 45.6 us (level)
  no operation moved by 1% of the time
where the time goes in v7:
time: 45.6 us; the launch traced here: 45.4 us
  Pallas kernels  44 us (96%)
  local copies, waits for them, and re-layouts  1.38 us (3%)
    pallas_call x1, Pallas kernels, per_device(): pl.pallas_call(kernel, out_shape=jax.ShapeDtypeStruct(design.shape, jnp.f...  44 us
    unnamed x1, local copies, waits for them, and re-layouts  1.38 us

profile of v7, /device:TPU:7, one launch (start us, length us, event | category | flops | bytes accessed | tf_op | source)
XLA Modules:
  0.0 45.4 jit_solution(6711769913468443653)
XLA Ops:
  0.0 44.0 %sensitivity.1 = f32[4,8,256]{2,1,0:T(8,128)} custom-call(f32[4,3,4,64,256]{4,3,2,1,0:T(8,128)} %disp.1, s32[4]{0:T(128)} %slot_node_in.1, f32[25]{0:T(128)} %node_weight_in.1, f32[25]{0:T(128)} %node_stiffness_in.1, f32[4,8,256]{2,1,0:T(8,128)} %design_in.1), custom_call_target="tpu_custom_call" | custom-call | flops 40000000 | bytes 4000000 | tf_op jit(solution)/shard_map/sensitivity/pallas_call | solution.py:533
  44.0 1.4 %copy.7 = f32[4,8,256]{2,1,0:T(8,128)} copy(f32[4,8,256]{2,1,0:T(8,128)} %sensitivity.1) | data formatting | bytes 65536

commit v8 on v7

--- a/solution.py
+++ b/solution.py
@@ -450,6 +450,15 @@
             span = pl.ds(first, 2)
             sen_pad[0, span, :] = jnp.where(cond & has_down, sen_cl[rim], 0.0)
             sen_pad[pl.ds(planes + 2, 2), span, :] = jnp.where(cond & has_up, sen_ch[rim], 0.0)
+        for copy, send_if, _ in started:
+            when(send_if, copy.wait_send)
+        for slot in range(half):
+            for way, where, send_if, *_ in ways:
+                pl.when(send_if)(slot_copy(way, slot, where).wait_send)
+        for way, where, _, _, _, crosses, _ in ways:
+            for (relay_way, plane, part), (at, stop) in slots_of.items():
+                if relay_way == way:
+                    pl.when(crosses & (place == at))(face_copy(way, plane, where, part, passed=stop).wait_send)
         arrive(late_halo)
         sen_pad[1, own, :] = jnp.where(has_down, late[0] + late_z[0], 0.0)
         sen_pad[planes + 1, own, :] = late[1] + jnp.where(has_up, late_z[1], 0.0)
@@ -463,16 +472,6 @@
         sens_rows = [row_sums(sen_pad, p) for p in range(planes + 4)]
         for plane in range(planes):
             out[plane] = smooth(z_sums(sens_rows, plane + 2), cols)
-
-        for copy, send_if, _ in started:
-            when(send_if, copy.wait_send)
-        for slot in range(half):
-            for way, where, send_if, *_ in ways:
-                pl.when(send_if)(slot_copy(way, slot, where).wait_send)
-        for way, where, _, _, _, crosses, _ in ways:
-            for (relay_way, plane, part), (at, stop) in slots_of.items():
-                if relay_way == way:
-                    pl.when(crosses & (place == at))(face_copy(way, plane, where, part, passed=stop).wait_send)
 
     vmem = lambda *shape: pltpu.VMEM(shape, jnp.float32)
     copies = 2 + 2 + 1 + 2 * chips + 6 + 8

time: 45.6 us -> 45.5 us (level)
  no operation moved by 1% of the time
where the time goes in v8:
time: 45.5 us; the launch traced here: 45.3 us
  Pallas kernels  43.9 us (96%)
  local copies, waits for them, and re-layouts  1.38 us (3%)
    pallas_call x1, Pallas kernels, per_device(): pl.pallas_call(kernel, out_shape=jax.ShapeDtypeStruct(design.shape, jnp.f...  43.9 us
    unnamed x1, local copies, waits for them, and re-layouts  1.38 us

profile of v8, /device:TPU:7, one launch (start us, length us, event | category | flops | bytes accessed | tf_op | source)
XLA Modules:
  0.0 45.3 jit_solution(14775586287061795674)
XLA Ops:
  0.0 43.9 %sensitivity.1 = f32[4,8,256]{2,1,0:T(8,128)} custom-call(f32[4,3,4,64,256]{4,3,2,1,0:T(8,128)} %disp.1, s32[4]{0:T(128)} %slot_node_in.1, f32[25]{0:T(128)} %node_weight_in.1, f32[25]{0:T(128)} %node_stiffness_in.1, f32[4,8,256]{2,1,0:T(8,128)} %design_in.1), custom_call_target="tpu_custom_call" | custom-call | flops 40000000 | bytes 4000000 | tf_op jit(solution)/shard_map/sensitivity/pallas_call | solution.py:532
  43.9 1.4 %copy.7 = f32[4,8,256]{2,1,0:T(8,128)} copy(f32[4,8,256]{2,1,0:T(8,128)} %sensitivity.1) | data formatting | bytes 65536
